TPU v7x, 512 devices: a whole 4x4x16 slice. The times are simulated.
512 devices in a mesh: gx: 64 (over z, y), gy: 8 (over x, core).
Axes of the slice: x: 4, y: 4, z: 16, core: 2. Of those that a mesh axis runs over, the one named last changes fastest.
Arguments:
- density: float32 [512, 192, 2048], P('gx', 'gy'), may hold values from 0.1 to 4
- centers: float32 [8], replicated, may hold values from 0.3 to 3.5
- widths: float32 [8], replicated, may hold values from 0.3 to 1.2
- weights: float32 [8], replicated, may hold values from 0.1 to 1
- colors: float32 [3, 8], replicated, may hold values from 0.2 to 2
- light: float32 [3], replicated, may hold values from -3 to 3
Outputs:
- image: float32 [4, 192, 2048], P(None, 'gy', 'gx')
All inputs are finite; a program needn't handle non-finite values.
Results may differ from a plain program's by a relative error of at most 0.00002.
Values sent between devices are 32-bit elements; how exact they have to be, the bound alone decides.
A program may use at most 64 MiB of HBM per device.

v0:
```python
import jax
import jax.numpy as jnp
from jax import lax
from jax.sharding import PartitionSpec as P


def padded_2(cells, sides, width):
    for axis, dim in sides:
        count = lax.axis_size(axis)
        ends = count - 1
        head = lax.slice_in_dim(cells, 0, width, axis=dim)
        tail = lax.slice_in_dim(cells, cells.shape[dim] - width, cells.shape[dim], axis=dim)
        cells = jnp.concatenate(
            [
                lax.ppermute(tail, axis, [(i, (i + 1) % count) for i in range(ends)]),
                cells,
                lax.ppermute(head, axis, [((i + 1) % count, i) for i in range(ends)]),
            ],
            axis=dim,
        )
    return cells


def prefix(part, axis, combine, identity):
    place = lax.axis_index(axis)
    gathered = lax.all_gather(part, axis)
    state = jnp.zeros_like(part) + jnp.asarray(identity, part.dtype)

    def one(step, state):
        return combine(state, lax.dynamic_index_in_dim(gathered, step, 0, False))

    return lax.fori_loop(0, place, one, state)


def sources(cells, grad_x, grad_y, grad_z, centers, widths, weights, colors, light):
    facing = light[0] * grad_x + light[1] * grad_y + light[2] * grad_z
    shading = 0.25 + 0.75 * jax.nn.sigmoid(2.0 * facing)
    extinction = jnp.zeros_like(cells)
    emitted = [jnp.zeros_like(cells) for channel in range(3)]
    for bump_index in range(centers.shape[0]):
        scaled = (cells - centers[bump_index]) / widths[bump_index]
        bump_value = jnp.exp(-scaled * scaled)
        extinction = extinction + weights[bump_index] * bump_value
        emitted = [
            emitted[channel] + colors[channel, bump_index] * bump_value for channel in range(3)
        ]
    return (extinction, [shading * source for source in emitted])


def march(cells, grad_x, grad_y, grad_z, centers, widths, weights, colors, light, step_size):
    extinction, emitted = sources(
        cells, grad_x, grad_y, grad_z, centers, widths, weights, colors, light
    )
    optical_step = step_size * extinction
    opacity = -jnp.expm1(-optical_step)
    before = jnp.cumsum(optical_step, axis=0) - optical_step
    weight = jnp.exp(-before) * opacity
    colour = jnp.stack([jnp.sum(weight * source, axis=0) for source in emitted])
    return (colour, jnp.sum(optical_step, axis=0))


def add_depth(earlier, later):
    return earlier + later


def local(density, centers, widths, weights, colors, light):
    step_size = 1.5 / (density.shape[0] * lax.axis_size("gx"))
    padded = padded_2(density, (("gx", 0), ("gy", 1)), 1)
    cells = padded[1:-1, 1:-1]
    grad_x = 0.5 * (padded[2:, 1:-1] - padded[:-2, 1:-1])
    grad_y = 0.5 * (padded[1:-1, 2:] - padded[1:-1, :-2])
    ahead = jnp.concatenate([cells[:, :, 1:], jnp.zeros_like(cells[:, :, :1])], 2)
    behind = jnp.concatenate([jnp.zeros_like(cells[:, :, :1]), cells[:, :, :-1]], 2)
    grad_z = 0.5 * (ahead - behind)
    colour, optical = march(
        cells, grad_x, grad_y, grad_z, centers, widths, weights, colors, light, step_size
    )
    before = prefix(optical, "gx", add_depth, jnp.zeros_like(optical))
    reach = jnp.exp(-before)
    terms = jnp.concatenate([reach[None] * colour, (reach * -jnp.expm1(-optical))[None]], 0)
    return lax.psum_scatter(terms, "gx", scatter_dimension=2, tiled=True)


def solution(mesh):
    in_specs = (P("gx", "gy", None), P(), P(), P(), P(), P())
    out_specs = P(None, "gy", "gx")
    return jax.shard_map(local, mesh=mesh, in_specs=in_specs, out_specs=out_specs, check_vma=False)
```

profile of v0, /device:TPU:6, one launch (start us, length us, event | category | flops | bytes accessed | tf_op | source)
XLA Modules:
  0.0 970.4 jit_solution(8699350199982270301)
XLA Ops:
  6.5 0.0 all-gather.3.cloned.1.call-start
  6.5 1.6 fusion.26
  8.2 1.6 fusion.27
  9.8 1.6 fusion.25
  11.4 0.0 copy-start
  11.4 21.8 %fusion.19 = (f32[24,2048]{1,0:T(8,128)}, f32[8,24,2048]{2,0,1:T(8,128)}) fusion(f32[]{:T(128)} %bitcast.26, f32[]{:T(128)} %bitcast.25, f32[]{:T(128)} %bitcast.24, f32[]{:T(128)} %bitcast.23, f32[]{:T(128)} %bitcast.22, f32[]{:T(128)} %bitcast.21, f32[]{:T(128)} %bitcast.20, f32[]{:T(128)} %bitcast.19, f32[]{:T(128)} %bitcast.18, f32[]{:T(128)} %bitcast.17, ...), kind=kLoop, calls=%fused_computation.49 | loop fusion | flops 19218432 | bytes 3342432 | tf_op jit(solution)/shard_map/reduce_sum | solution.py:59
  33.2 0.0 all-gather.3.cloned.1.call-update
  33.2 0.0 reduce-scatter.4.cloned.1.call-start
  33.2 0.0 copy-done
  33.3 0.8 fusion.20
  34.0 1.3 collective-permute-start
  35.3 4.6 collective-permute-start.1
  39.9 0.9 copy.22
  40.8 0.0 copy-start.5
  40.8 2.2 fusion.21
  43.0 0.0 copy-done.5
  43.0 0.6 fusion.24
  45.5 0.0 copy-start.4
  45.5 5.1 reduce_window_sum.11
  50.5 0.0 copy-done.4
  50.5 0.0 copy-start.1
  50.6 0.7 fusion.22
  51.3 0.0 collective-permute-done
  51.3 0.2 copy.31
  51.5 0.0 collective-permute-done.1
  51.5 0.2 copy.32
  51.7 0.1 pad_maximum_fusion.11
  51.8 1.9 collective-permute-start.2
  53.7 2.6 collective-permute-start.3
  56.3 0.7 fusion.23
  57.0 0.0 collective-permute-done.2
  57.0 3.0 collective-permute-done.3
  60.0 0.0 copy-done.1
  60.0 0.0 copy-start.2
  60.0 23.2 %multiply_reduce_fusion.2 = (f32[24,2048]{1,0:T(8,128)S(1)}, f32[8,24,2048]{2,0,1:T(8,128)S(1)}) fusion(f32[]{:T(128)} %bitcast.38, f32[]{:T(128)} %bitcast.37, f32[]{:T(128)} %bitcast.36, f32[]{:T(128)} %bitcast.35, f32[]{:T(128)} %bitcast.34, f32[]{:T(128)} %bitcast.33, f32[]{:T(128)} %bitcast.32, f32[]{:T(128)} %bitcast.31, ...), kind=kLoop, calls=%fused_computation.38 | loop fusion | flops 30228480 | bytes 11762284 | tf_op jit(solution)/shard_map/reduce_sum | solution.py:58
  83.2 0.0 copy-done.2
  83.2 19.9 %multiply_reduce_fusion.1 = f32[24,2048]{1,0:T(8,128)S(1)} fusion(f32[8,24,2048]{2,0,1:T(8,128)S(1)} %get-tuple-element.38, f32[]{:T(128)} %bitcast.47, f32[]{:T(128)} %bitcast.46, f32[]{:T(128)} %bitcast.45, f32[]{:T(128)} %bitcast.44, f32[]{:T(128)} %bitcast.43, f32[]{:T(128)} %bitcast.42, f32[]{:T(128)} %bitcast.41, f32[]{:T(128)} %bitcast.40, ...), kind=kLoop, calls=%fused_computation.37 | loop fusion | flops 21577728 | bytes 6488160 | tf_op jit(solution)/shard_map/reduce_sum | solution.py:58
  103.1 19.8 %multiply_reduce_fusion = f32[24,2048]{1,0:T(8,128)S(1)} fusion(f32[8,24,2048]{2,0,1:T(8,128)S(1)} %get-tuple-element.38, f32[]{:T(128)} %bitcast.56, f32[]{:T(128)} %bitcast.55, f32[]{:T(128)} %bitcast.54, f32[]{:T(128)} %bitcast.53, f32[]{:T(128)} %bitcast.52, f32[]{:T(128)} %bitcast.51, f32[]{:T(128)} %bitcast.50, f32[]{:T(128)} %bitcast.49, ...), kind=kLoop, calls=%fused_computation.36 | loop fusion | flops 21577728 | bytes 6488160 | tf_op jit(solution)/shard_map/reduce_sum | solution.py:58
  123.0 85.9 %all-gather.3.cloned.1.call-done = f32[1536,2048]{1,0:T(8,128)} async-done(((f32[24,2048]{1,0:T(8,128)}), f32[1536,2048]{1,0:T(8,128)}) %all-gather.3.cloned.1.call-update) | async-done | bytes 12582928 | tf_op jit(solution)/shard_map/all_gather | solution.py:26
  208.9 0.0 copy-start.3
  208.9 0.9 copy-done.3
  209.8 0.1 negate_exponential_fusion
  209.9 0.1 maximum_multiply_fusion
  210.0 0.1 pad_maximum_fusion.8
  210.1 3.1 copy.39
  213.2 4.5 reshape.8
  217.7 0.0 reduce-scatter.4.cloned.1.call-update
  217.7 744.3 %reduce-scatter.4.cloned.1.call-done = f32[32,96]{1,0:T(8,128)} async-done(((f32[2048,96]{1,0:T(8,128)}), f32[32,96]{1,0:T(8,128)}) %reduce-scatter.4.cloned.1.call-update) | async-done | bytes 12304
  962.0 0.8 reshape.9
  962.8 0.7 copy.40
  (2 shorter events, 0.0 us)
Async XLA Ops:
  6.5 202.4 %all-gather.3.cloned.1.call-start = ((), (), s32[]{:S(2)}) async-start(), calls=%async_computation.1 | async-start | bytes 12779520 | tf_op jit(solution)/shard_map/all_gather | solution.py:26
  11.4 21.8 %copy-start = (f32[8,24,2048]{2,1,0:T(8,128)S(1)}, f32[8,24,2048]{2,1,0:T(8,128)}, u32[]{:S(2)}) copy-start(f32[8,24,2048]{2,1,0:T(8,128)} %param.8) | copy-start | bytes 4718596
  33.2 928.8 %reduce-scatter.4.cloned.1.call-start = ((), (), s32[]{:S(2)}) async-start(), calls=%async_computation.2 | async-start | bytes 1064960
  34.0 17.2 %collective-permute-start = (f32[1,24,2048]{2,1,0:T(8,128)}, f32[1,24,2048]{2,1,0:T(8,128)S(1)}, u32[]{:S(2)}, u32[]{:S(2)}) collective-permute-start(f32[1,24,2048]{2,1,0:T(8,128)} %get-tuple-element.44), channel_id=1, source_target_pairs={{8,0},{16,8},{24,16},{32,24},{40,32},{48,40},{56,48},{64,56},{72,6... | collective-permute-start | bytes 589832 | tf_op jit(solution)/shard_map/ppermute | solution.py:17
  35.3 16.2 %collective-permute-start.1 = (f32[1,24,2048]{2,1,0:T(8,128)}, f32[1,24,2048]{2,1,0:T(8,128)S(1)}, u32[]{:S(2)}, u32[]{:S(2)}) collective-permute-start(f32[1,24,2048]{2,1,0:T(8,128)} %get-tuple-element.43), channel_id=1, source_target_pairs={{0,8},{8,16},{16,24},{24,32},{32,40},{40,48},{48,56},{56,64},{64,7... | collective-permute-start | bytes 589832 | tf_op jit(solution)/shard_map/ppermute | solution.py:15
  40.8 2.2 copy-start.5
  45.5 5.1 copy-start.4
  50.5 9.4 copy-start.1
  51.8 5.2 collective-permute-start.2
  53.7 6.3 collective-permute-start.3
  60.0 23.2 %copy-start.2 = (f32[8,24,2048]{2,0,1:T(8,128)S(1)}, f32[8,24,2048]{2,0,1:T(8,128)}, u32[]{:S(2)}) copy-start(f32[8,24,2048]{2,0,1:T(8,128)} %reduce_window_sum.11) | copy-start | bytes 4718596
  208.9 0.9 copy-start.3
Sparse Core Ops, SparseCore 0:
  33.3 175.5 all-gather.2
  217.8 744.1 reduce-scatter.3
where the time goes:
time: 973 us; the launch traced here: 970 us
  waiting for transfers between devices  833 us (86%)
  other arithmetic  90 us (9%)
  local copies, waits for them, and re-layouts  21.3 us (2%)
  between operations  15.4 us (2%)
  starting transfers between devices  10.4 us (1%)
    unnamed x3, waiting for transfers between devices  744 us
    all_gather x1, waiting for transfers between devices, prefix(): gathered = lax.all_gather(part, axis)  85.9 us
    reduce_sum x3, other arithmetic, march(): colour = jnp.stack([jnp.sum(weight * source, axis=0) for source in emitted])  63 us
    reduce_sum x1, other arithmetic, march(): return (colour, jnp.sum(optical_step, axis=0))  21.8 us
  transfers between devices with their start and end apart: 6, of which 3 were waited for; matrix products, arithmetic and copies ran while one was open for 8% of the time, Pallas kernels for 0%

commit v1 on v0

v1 whole, which is shorter than its diff:
```python
import functools
import math

import jax
import jax.numpy as jnp
from jax import lax
from jax.experimental import pallas as pl
from jax.experimental.pallas import tpu as pltpu
from jax.sharding import PartitionSpec as P

MESH = pl.DeviceIdType.MESH
LANES = 128
Q = 4
G = LANES // Q
PARTS = 4
SUB = 256


def roll_lanes(v, by):
    return pltpu.roll(v, by % LANES, axis=1)


def shifted(tiles, by, edge, lane_or_row, axis):
    size = tiles[0].shape[axis]
    rolled = [pltpu.roll(t, by % size, axis=axis) for t in tiles]
    if by > 0:
        before = [edge] + rolled[:-1]
        return [jnp.where(lane_or_row == 0, b, r) for b, r in zip(before, rolled)]
    after = rolled[1:] + [edge]
    return [jnp.where(lane_or_row == size - 1, a, r) for a, r in zip(after, rolled)]


def regroup(values, lane):
    a, b, c, d = values
    low = lane < 2 * G
    ac0 = jnp.where(low, a, roll_lanes(c, 2 * G))
    ac1 = jnp.where(low, roll_lanes(a, -2 * G), c)
    bd0 = jnp.where(low, b, roll_lanes(d, 2 * G))
    bd1 = jnp.where(low, roll_lanes(b, -2 * G), d)
    even = lax.rem(lane // G, 2) == 0
    out = []
    for first, second in ((ac0, bd0), (ac1, bd1)):
        out.append(jnp.where(even, first, roll_lanes(second, G)))
        out.append(jnp.where(even, roll_lanes(first, -G), second))
    return out


def over(front, back, lane):
    clear = 1.0 - front
    ends = jnp.where(lane < G, roll_lanes(clear, G), clear)
    inner = (lane >= G) & (lane < 3 * G)
    return front + jnp.where(inner, roll_lanes(ends, 2 * G), ends) * back


def kernel(
    nx, ny, step_size, density, centers, widths, weights, colors, light, out,
    x, rows_out, rows_in, depth_in, prm, emi, p1s, p1r, p2s, p2r,
    x_sem, rows_ss, rows_rs, depth_ss, depth_rs, p1_ss, p1_rs, p2_ss, p2_rs,
):
    layers, rows, cols = density.shape
    nz = nx // Q
    bumps = centers.shape[0]
    width = cols // PARTS
    per = width // LANES
    me, my = lax.axis_index("gx"), lax.axis_index("gy")
    z, y = me // Q, lax.rem(me, Q)
    nxt, prv = lax.rem(me + 1, nx), lax.rem(me + nx - 1, nx)
    down, up = lax.rem(my + 1, ny), lax.rem(my + ny - 1, ny)

    load = pltpu.make_async_copy(density, x.at[:, :, pl.ds(LANES, cols)], x_sem)
    load.start()

    barrier = pltpu.get_barrier_semaphore()

    def greet(gx, gy):
        pl.semaphore_signal(barrier, inc=1, device_id=(gx, gy), device_id_type=MESH)

    greet(nxt, my)
    greet(prv, my)
    greet(me, down)
    greet(me, up)

    def greet_y(k, _):
        greet(z * Q + lax.rem(y + k, Q), my)
        return 0

    def greet_z(k, _):
        greet(lax.rem(z + k, nz) * Q + y, my)
        return 0

    lax.fori_loop(1, Q, greet_y, 0)
    lax.fori_loop(1, nz, greet_z, 0)

    tile = (8, LANES)
    scale = math.sqrt(math.log2(math.e))
    for k in range(bumps):
        weight = jnp.full(tile, weights[k] * step_size, jnp.float32)
        prm[6 * k] = jnp.full(tile, centers[k], jnp.float32)
        prm[6 * k + 1] = scale / jnp.full(tile, widths[k], jnp.float32)
        prm[6 * k + 2] = jnp.log2(weight)
        for c in range(3):
            prm[6 * k + 3 + c] = jnp.full(tile, colors[c, k], jnp.float32) / weight
    for c in range(3):
        prm[6 * bumps + c] = jnp.full(tile, 0.5 * light[c], jnp.float32)
    x[:, :, :LANES] = jnp.zeros((layers, rows, LANES), jnp.float32)
    x[:, :, LANES + cols :] = jnp.zeros((layers, rows, LANES), jnp.float32)

    load.wait()
    for l in range(layers):
        rows_out[0, l : l + 1, :] = x[l, 0:1, LANES : LANES + cols]
        rows_out[1, l : l + 1, :] = x[l, rows - 1 : rows, LANES : LANES + cols]

    def part_at(s, place):
        return lax.rem(place // Q + jnp.where(s == 0, 2, jnp.where(s == 1, 1, jnp.where(s == 2, 3, 0))), PARTS)

    def rows_copy(side, s):
        at = pl.ds(pl.multiple_of(part_at(s, z) * width, width), width)
        return pltpu.make_async_remote_copy(
            src_ref=rows_out.at[1 - side, :, at],
            dst_ref=rows_in.at[side, :, at],
            send_sem=rows_ss.at[side, s],
            recv_sem=rows_rs.at[side, s],
            device_id=(me, down if side == 0 else up),
            device_id_type=MESH,
        )

    def depth_copy(side, s, place, gx):
        start = pl.multiple_of(part_at(s, place) * width, width)
        return pltpu.make_async_remote_copy(
            src_ref=x.at[layers - 1 if side == 0 else 0, :, pl.ds(pl.multiple_of(start + LANES, LANES), width)],
            dst_ref=depth_in.at[side, :, pl.ds(start, width)],
            send_sem=depth_ss.at[side, s],
            recv_sem=depth_rs.at[side, s],
            device_id=(gx, my),
            device_id_type=MESH,
        )

    def p1_copy(s, k):
        to = lax.rem(y + k, Q)
        return pltpu.make_async_remote_copy(
            src_ref=p1s.at[s, to],
            dst_ref=p1r.at[s, k],
            send_sem=p1_ss.at[s, k],
            recv_sem=p1_rs.at[s, k],
            device_id=(z * Q + to, my),
            device_id_type=MESH,
        )

    def p2_copy(to):
        k = lax.rem(to + nz - z, nz)
        return pltpu.make_async_remote_copy(
            src_ref=p2s.at[to],
            dst_ref=p2r.at[k],
            send_sem=p2_ss.at[k],
            recv_sem=p2_rs.at[k],
            device_id=(to * Q + y, my),
            device_id_type=MESH,
        )

    pl.semaphore_wait(barrier, 4 + (Q - 1) + (nz - 1))

    def send_halos(s, _):
        for side in range(2):
            rows_copy(side, s).start()
        depth_copy(0, s, nxt // Q, nxt).start()
        depth_copy(1, s, prv // Q, prv).start()
        return 0

    lax.fori_loop(0, PARTS, send_halos, 0)

    lane = lax.broadcasted_iota(jnp.int32, tile, 1)
    row = lax.broadcasted_iota(jnp.int32, tile, 0)
    lane_all = lax.broadcasted_iota(jnp.int32, (rows, LANES), 1)
    lane_part = lax.broadcasted_iota(jnp.int32, (per, rows, LANES), 2)
    from_prv = jnp.where(me > 0, 1.0, 0.0).astype(jnp.float32)
    from_nxt = jnp.where(me < nx - 1, 1.0, 0.0).astype(jnp.float32)
    from_up = jnp.where(my > 0, 1.0, 0.0).astype(jnp.float32)
    from_down = jnp.where(my < ny - 1, 1.0, 0.0).astype(jnp.float32)
    reps = (rows // 8, SUB // LANES)

    def wide(i):
        return jnp.tile(prm[i], reps)

    def emit(part):
        def one(i, _):
            l, start = lax.rem(i, layers), (i // layers) * SUB
            cells = x[l, :, pl.ds(pl.multiple_of(part * width + start + LANES, LANES), SUB)]
            sums = None
            for k in range(bumps):
                scaled = (cells - wide(6 * k)) * wide(6 * k + 1)
                step = jnp.exp2(wide(6 * k + 2) - scaled * scaled)
                terms = [step] + [step * wide(6 * k + 3 + c) for c in range(3)]
                sums = terms if sums is None else [a + b for a, b in zip(sums, terms)]
            t = sums[0]
            opacity = t * (1.0 - t * (0.5 - t * (1.0 / 6.0 - t * (1.0 / 24.0))))
            at = pl.ds(pl.multiple_of(start, SUB), SUB)
            for c, v in enumerate([opacity] + sums[1:]):
                emi[c, l, :, at] = v
            return 0

        lax.fori_loop(0, layers * (width // SUB), one, 0)

    n_lane, n_row = SUB // LANES, rows // 8

    def grid_of(v):
        return [[v[8 * r : 8 * r + 8, LANES * c : LANES * c + LANES] for c in range(v.shape[1] // LANES)] for r in range(v.shape[0] // 8)]

    def joined(tiles):
        return jnp.concatenate([jnp.concatenate(line, 1) for line in tiles], 0)

    def march(s, part):
        def one(i, _):
            at = pl.multiple_of(part * width + i * SUB, SUB)
            here = pl.ds(pl.multiple_of(i * SUB, SUB), SUB)
            hx, hy, hz = (wide(6 * bumps + c) for c in range(3))
            clear = jnp.ones((rows, SUB), jnp.float32)
            opaque = jnp.zeros((rows, SUB), jnp.float32)
            colour = [jnp.zeros((rows, SUB), jnp.float32) for c in range(3)]

            def layer(l):
                return x[l, :, pl.ds(pl.multiple_of(at + LANES, LANES), SUB)]

            before, cells = depth_in[0, :, pl.ds(at, SUB)] * from_prv, layer(0)
            for l in range(layers):
                after = layer(l + 1) if l < layers - 1 else depth_in[1, :, pl.ds(at, SUB)] * from_nxt
                tiles = grid_of(cells)
                left = grid_of(x[l, :, pl.ds(at, LANES)])
                right = grid_of(x[l, :, pl.ds(pl.multiple_of(at + LANES + SUB, LANES), LANES)])
                behind = [shifted(tiles[r], 1, roll_lanes(left[r][0], 1), lane, 1) for r in range(n_row)]
                ahead = [shifted(tiles[r], -1, roll_lanes(right[r][0], -1), lane, 1) for r in range(n_row)]
                over_row = jnp.broadcast_to(rows_in[0, l : l + 1, pl.ds(at, SUB)], (8, SUB)) * from_up
                under_row = jnp.broadcast_to(rows_in[1, l : l + 1, pl.ds(at, SUB)], (8, SUB)) * from_down
                above, below = [], []
                for c in range(n_lane):
                    column = [tiles[r][c] for r in range(n_row)]
                    above.append(shifted(column, 1, over_row[:, LANES * c : LANES * c + LANES], row, 0))
                    below.append(shifted(column, -1, under_row[:, LANES * c : LANES * c + LANES], row, 0))
                above = [[above[c][r] for c in range(n_lane)] for r in range(n_row)]
                below = [[below[c][r] for c in range(n_lane)] for r in range(n_row)]
                facing = (
                    hx * (after - before)
                    + hy * (joined(below) - joined(above))
                    + hz * (joined(ahead) - joined(behind))
                )
                shading = 0.625 + 0.375 * jnp.tanh(facing)
                seen = clear * emi[0, l, :, here]
                clear, opaque = clear - seen, opaque + seen
                lit = seen * shading
                colour = [colour[c] + lit * emi[c + 1, l, :, here] for c in range(3)]
                before, cells = cells, after
            for b in range(n_lane):
                cut = slice(LANES * b, LANES * b + LANES)
                owned = regroup([v[:, cut] for v in colour + [opaque]], lane_all)
                for j in range(Q):
                    p1s[s, j, i * n_lane + b] = owned[j]
            return 0

        lax.fori_loop(0, width // SUB, one, 0)

    def step(s, _):
        @pl.when(s < PARTS)
        def _():
            part = part_at(s, z)
            emit(part)
            for side in range(2):
                rows_copy(side, s).wait_recv()
                depth_copy(side, s, z, (nxt, prv)[side]).wait_recv()
            march(s, part)
            for k in (2, 1, 3):
                p1_copy(s, k).start()

        @pl.when(s > 0)
        def _():
            t = s - 1
            part = part_at(t, z)
            p1r[t, 0] = p1s[t, y]
            for k in range(1, Q):
                p1_copy(t, k).wait_recv()
            total = p1r[t, lax.rem(y + 1, Q)]
            for j in range(Q - 2, -1, -1):
                total = over(p1r[t, lax.rem(y + Q - j, Q)].reshape(per * rows, LANES), total.reshape(per * rows, LANES), lane_flat)
            total = total.reshape(per, rows, LANES)
            for b in range(per):
                to = part * per + b
                p2s[to] = total[b]

                @pl.when(to != z)
                def _():
                    p2_copy(to).start()

        return 0

    lane_flat = lax.broadcasted_iota(jnp.int32, (per * rows, LANES), 1)
    lax.fori_loop(0, PARTS + 1, step, 0)

    p2r[0] = p2s[z]

    def wait_p2(k, _):
        p2_copy(lax.rem(z + k, nz)).wait_recv()
        return 0

    lax.fori_loop(1, nz, wait_p2, 0)

    def behind_all(i, total):
        return over(p2r[lax.rem(z + 1 + i, nz)], total, lane_all)

    total = lax.fori_loop(1, nz, behind_all, p2r[lax.rem(z + 1, nz)])
    for c in range(4):
        out[c] = total[:, G * c : G * c + G]

    def finish_halos(s, _):
        for side in range(2):
            rows_copy(side, s).wait_send()
            depth_copy(side, s, z, (nxt, prv)[side]).wait_send()
        for k in range(1, Q):
            p1_copy(s, k).wait_send()
        return 0

    lax.fori_loop(0, PARTS, finish_halos, 0)

    def finish_p2(k, _):
        p2_copy(lax.rem(z + k, nz)).wait_send()
        return 0

    lax.fori_loop(1, nz, finish_p2, 0)


def local(nx, ny, density, centers, widths, weights, colors, light):
    layers, rows, cols = density.shape
    nz, bumps = nx // Q, centers.shape[0]
    width = cols // PARTS
    per = width // LANES
    dma = pltpu.SemaphoreType.DMA
    smem = pl.BlockSpec(memory_space=pltpu.SMEM)
    f32 = jnp.float32
    return pl.pallas_call(
        functools.partial(kernel, nx, ny, 1.5 / (layers * nx)),
        out_shape=jax.ShapeDtypeStruct((4, rows, cols // nx), f32),
        in_specs=[pl.BlockSpec(memory_space=pl.ANY)] + [smem] * 5,
        out_specs=pl.BlockSpec(memory_space=pltpu.VMEM),
        scratch_shapes=[
            pltpu.VMEM((layers, rows, cols + 2 * LANES), f32),
            pltpu.VMEM((2, layers, cols), f32),
            pltpu.VMEM((2, layers, cols), f32),
            pltpu.VMEM((2, rows, cols), f32),
            pltpu.VMEM((6 * bumps + 3, 8, LANES), f32),
            pltpu.VMEM((4, layers, rows, width), f32),
            pltpu.VMEM((PARTS, Q, per, rows, LANES), f32),
            pltpu.VMEM((PARTS, Q, per, rows, LANES), f32),
            pltpu.VMEM((nz, rows, LANES), f32),
            pltpu.VMEM((nz, rows, LANES), f32),
            dma,
            dma((2, PARTS)),
            dma((2, PARTS)),
            dma((2, PARTS)),
            dma((2, PARTS)),
            dma((PARTS, Q)),
            dma((PARTS, Q)),
            dma((nz,)),
            dma((nz,)),
        ],
        compiler_params=pltpu.CompilerParams(
            collective_id=0, has_side_effects=True, vmem_limit_bytes=40 * 1024 * 1024
        ),
        cost_estimate=pl.CostEstimate(
            flops=130 * density.size, bytes_accessed=4 * density.size, transcendentals=9 * density.size
        ),
    )(density, centers, widths, weights, colors, light)


def solution(mesh):
    nx, ny = mesh.shape["gx"], mesh.shape["gy"]
    in_specs = (P("gx", "gy", None), P(), P(), P(), P(), P())
    out_specs = P(None, "gy", "gx")
    return jax.shard_map(
        functools.partial(local, nx, ny), mesh=mesh, in_specs=in_specs, out_specs=out_specs, check_vma=False
    )
```

time: 973 us -> 49.5 us (0.05)
  waiting for transfers between devices: 833 us -> 0 us
  other arithmetic: 90 us -> 0 us
  Pallas kernels: 0 us -> 44 us
  local copies, waits for them, and re-layouts: 21.3 us -> 5.33 us
  between operations: 15.4 us -> 0.02 us
  starting transfers between devices: 10.4 us -> 0 us
    unnamed x3 -> x0, waiting for transfers between devices: 744 us -> none
    all_gather x1 -> x0, waiting for transfers between devices: 85.9 us -> none  [prefix(): gathered = lax.all_gather(part, axis)]
    reduce_sum x4 -> x0, other arithmetic: 84.7 us -> none  [the longest x3 63 us: march(): colour = jnp.stack([jnp.sum(weight * source, axis=0) for source in emitted])]
    pallas_call x0 -> x1, Pallas kernels: none -> 44 us  [local(): pl.pallas_call(functools.partial(kernel, nx, ny, 1.5 / (layers * nx)), ou...]
    ppermute x4 -> x0, starting transfers between devices: 10.3 us -> none  [the longest x2 7.15 us: padded_2(): lax.ppermute(tail, axis, [(i, (i + 1) % count) for i in range(ends)])]
    slice x8 -> x0, local copies, waits for them, and re-layouts: 9.86 us -> none  [the longest x2 3.26 us: sources(): scaled = (cells - centers[bump_index]) / widths[bump_index]]
  transfers between devices with their start and end apart: 6 -> 0, of which waited for: 3 -> 0; matrix products, arithmetic and copies ran while one was open for 8% -> 0% of each run, Pallas kernels for 0% -> 0%
where the time goes in v1:
time: 49.5 us; the launch traced here: 49.3 us
  Pallas kernels  44 us (89%)
  local copies, waits for them, and re-layouts  5.33 us (11%)
    pallas_call x1, Pallas kernels, local(): pl.pallas_call(functools.partial(kernel, nx, ny, 1.5 / (layers * nx)), ou...  44 us
    unnamed x13, local copies, waits for them, and re-layouts  5.33 us

profile of v1, /device:TPU:6, one launch (start us, length us, event | category | flops | bytes accessed | tf_op | source)
XLA Modules:
  0.0 49.3 jit_solution(3286209411613655464)
XLA Ops:
  0.0 0.0 copy-start
  0.0 1.4 %copy-done = f32[8,24,2048]{2,1,0:T(8,128)S(1)} copy-done((f32[8,24,2048]{2,1,0:T(8,128)S(1)}, f32[8,24,2048]{2,1,0:T(8,128)}, u32[]{:S(2)}) %copy-start) | copy-done | bytes 1572888
  1.4 0.0 copy-start.1
  1.4 0.7 %copy-done.1 = f32[3,8]{1,0:T(4,128)S(1)} copy-done((f32[3,8]{1,0:T(4,128)S(1)}, f32[3,8]{1,0:T(4,128)}, u32[]{:S(2)}) %copy-start.1) | copy-done | bytes 120
  2.1 0.0 copy-start.2
  2.1 0.7 %copy-done.2 = f32[8]{0:T(128)S(1)} copy-done((f32[8]{0:T(128)S(1)}, f32[8]{0:T(128)}, u32[]{:S(2)}) %copy-start.2) | copy-done | bytes 56
  2.7 0.0 copy-start.3
  2.7 0.7 %copy-done.3 = f32[8]{0:T(128)S(1)} copy-done((f32[8]{0:T(128)S(1)}, f32[8]{0:T(128)}, u32[]{:S(2)}) %copy-start.3) | copy-done | bytes 56
  3.4 0.0 copy-start.4
  3.4 0.7 %copy-done.4 = f32[8]{0:T(128)S(1)} copy-done((f32[8]{0:T(128)S(1)}, f32[8]{0:T(128)}, u32[]{:S(2)}) %copy-start.4) | copy-done | bytes 56
  4.1 0.0 copy-start.5
  4.1 0.7 %copy-done.5 = f32[3]{0:T(128)S(1)} copy-done((f32[3]{0:T(128)S(1)}, f32[3]{0:T(128)}, u32[]{:S(2)}) %copy-start.5) | copy-done | bytes 36
  4.7 44.0 %shard_map.64 = f32[4,24,32]{2,1,0:T(8,128)S(1)} custom-call(f32[8,24,2048]{2,1,0:T(8,128)S(1)} %copy-done, f32[8]{0:T(128)S(1)} %copy-done.2, f32[8]{0:T(128)S(1)} %copy-done.3, f32[8]{0:T(128)S(1)} %copy-done.4, f32[3,8]{1,0:T(4,128)S(1)} %copy-done.1, f32[3]{0:T(128)S(1)} %copy-done.5), custom_call_target="tpu_custom_call" | custom-call | flops 51118080 | bytes 1572864 | tf_op jit(solution)/shard_map/pallas_call | solution.py:336
  48.7 0.6 %copy.8 = f32[4,24,32]{2,1,0:T(8,128)} copy(f32[4,24,32]{2,1,0:T(8,128)S(1)} %shard_map.64) | data formatting | bytes 24576
Async XLA Ops:
  0.0 1.4 %copy-start = (f32[8,24,2048]{2,1,0:T(8,128)S(1)}, f32[8,24,2048]{2,1,0:T(8,128)}, u32[]{:S(2)}) copy-start(f32[8,24,2048]{2,1,0:T(8,128)} %density.1) | copy-start | bytes 4718596
  1.4 0.7 %copy-start.1 = (f32[3,8]{1,0:T(4,128)S(1)}, f32[3,8]{1,0:T(4,128)}, u32[]{:S(2)}) copy-start(f32[3,8]{1,0:T(4,128)} %colors.1) | copy-start | bytes 292
  2.1 0.7 %copy-start.2 = (f32[8]{0:T(128)S(1)}, f32[8]{0:T(128)}, u32[]{:S(2)}) copy-start(f32[8]{0:T(128)} %centers.1) | copy-start | bytes 100
  2.7 0.7 %copy-start.3 = (f32[8]{0:T(128)S(1)}, f32[8]{0:T(128)}, u32[]{:S(2)}) copy-start(f32[8]{0:T(128)} %widths.1) | copy-start | bytes 100
  3.4 0.7 %copy-start.4 = (f32[8]{0:T(128)S(1)}, f32[8]{0:T(128)}, u32[]{:S(2)}) copy-start(f32[8]{0:T(128)} %weights.1) | copy-start | bytes 100
  4.1 0.7 %copy-start.5 = (f32[3]{0:T(128)S(1)}, f32[3]{0:T(128)}, u32[]{:S(2)}) copy-start(f32[3]{0:T(128)} %light.1) | copy-start | bytes 40

commit v2 on v1

--- a/solution.py
+++ b/solution.py
@@ -12,7 +12,7 @@
 LANES = 128
 Q = 4
 G = LANES // Q
-PARTS = 4
+PARTS = 8
 SUB = 256
 
 
@@ -53,10 +53,12 @@
 
 
 def kernel(
-    nx, ny, step_size, density, centers, widths, weights, colors, light, out,
-    x, rows_out, rows_in, depth_in, prm, emi, p1s, p1r, p2s, p2r,
-    x_sem, rows_ss, rows_rs, depth_ss, depth_rs, p1_ss, p1_rs, p2_ss, p2_rs,
+    nx, ny, step_size, density, *rest,
 ):
+    given, rest = rest[:5], rest[5:]
+    out, centers, widths, weights, colors, light = rest[:6]
+    x, rows_out, rows_in, depth_in, prm, emi, p1s, p1r, pair, r1r, p2s, p2r = rest[6:18]
+    x_sem, given_sem, rows_ss, rows_rs, depth_ss, depth_rs, p1_ss, p1_rs, r1_ss, r1_rs, p2_ss, p2_rs = rest[18:]
     layers, rows, cols = density.shape
     nz = nx // Q
     bumps = centers.shape[0]
@@ -64,11 +66,20 @@
     per = width // LANES
     me, my = lax.axis_index("gx"), lax.axis_index("gy")
     z, y = me // Q, lax.rem(me, Q)
+    partner, mirror = y + 1 - 2 * lax.rem(y, 2), Q - 1 - y
+    kept = jnp.where((y == 0) | (y == Q - 1), 0, 2)
+    own = y // 2
     nxt, prv = lax.rem(me + 1, nx), lax.rem(me + nx - 1, nx)
     down, up = lax.rem(my + 1, ny), lax.rem(my + ny - 1, ny)
 
     load = pltpu.make_async_copy(density, x.at[:, :, pl.ds(LANES, cols)], x_sem)
     load.start()
+    fetches = [
+        pltpu.make_async_copy(src, dst, given_sem.at[i])
+        for i, (src, dst) in enumerate(zip(given, (centers, widths, weights, colors, light)))
+    ]
+    for fetch in fetches:
+        fetch.start()
 
     barrier = pltpu.get_barrier_semaphore()
 
@@ -80,17 +91,74 @@
     greet(me, down)
     greet(me, up)
 
-    def greet_y(k, _):
-        greet(z * Q + lax.rem(y + k, Q), my)
-        return 0
-
     def greet_z(k, _):
         greet(lax.rem(z + k, nz) * Q + y, my)
         return 0
 
-    lax.fori_loop(1, Q, greet_y, 0)
+    greet(z * Q + partner, my)
+    greet(z * Q + mirror, my)
     lax.fori_loop(1, nz, greet_z, 0)
-
+    x[:, :, :LANES] = jnp.zeros((layers, rows, LANES), jnp.float32)
+    x[:, :, LANES + cols :] = jnp.zeros((layers, rows, LANES), jnp.float32)
+
+    def part_at(s, place):
+        away = jnp.where(lax.rem(s, 2) == 0, s // 2, PARTS - (s + 1) // 2)
+        return lax.rem(place // per + PARTS // 2 + away, PARTS)
+
+    def rows_copy(side):
+        return pltpu.make_async_remote_copy(
+            src_ref=rows_out.at[1 - side],
+            dst_ref=rows_in.at[side],
+            send_sem=rows_ss.at[side],
+            recv_sem=rows_rs.at[side],
+            device_id=(me, down if side == 0 else up),
+            device_id_type=MESH,
+        )
+
+    def depth_copy(side, s, place, gx):
+        start = pl.multiple_of(part_at(s, place) * width, width)
+        return pltpu.make_async_remote_copy(
+            src_ref=density.at[layers - 1 if side == 0 else 0, :, pl.ds(start, width)],
+            dst_ref=depth_in.at[side, :, pl.ds(start, width)],
+            send_sem=depth_ss.at[side, s],
+            recv_sem=depth_rs.at[side, s],
+            device_id=(gx, my),
+            device_id_type=MESH,
+        )
+
+    def p1_copy(s):
+        return pltpu.make_async_remote_copy(
+            src_ref=p1s.at[s, pl.ds(2 - kept, 2)],
+            dst_ref=p1r.at[s],
+            send_sem=p1_ss.at[s],
+            recv_sem=p1_rs.at[s],
+            device_id=(z * Q + partner, my),
+            device_id_type=MESH,
+        )
+
+    def r1_copy(s):
+        return pltpu.make_async_remote_copy(
+            src_ref=pair.at[s, 1 - own],
+            dst_ref=r1r.at[s],
+            send_sem=r1_ss.at[s],
+            recv_sem=r1_rs.at[s],
+            device_id=(z * Q + mirror, my),
+            device_id_type=MESH,
+        )
+
+    def p2_copy(to):
+        k = lax.rem(to + nz - z, nz)
+        return pltpu.make_async_remote_copy(
+            src_ref=p2s.at[to],
+            dst_ref=p2r.at[k],
+            send_sem=p2_ss.at[k],
+            recv_sem=p2_rs.at[k],
+            device_id=(to * Q + y, my),
+            device_id_type=MESH,
+        )
+
+    for fetch in fetches:
+        fetch.wait()
     tile = (8, LANES)
     scale = math.sqrt(math.log2(math.e))
     for k in range(bumps):
@@ -102,76 +170,26 @@
             prm[6 * k + 3 + c] = jnp.full(tile, colors[c, k], jnp.float32) / weight
     for c in range(3):
         prm[6 * bumps + c] = jnp.full(tile, 0.5 * light[c], jnp.float32)
-    x[:, :, :LANES] = jnp.zeros((layers, rows, LANES), jnp.float32)
-    x[:, :, LANES + cols :] = jnp.zeros((layers, rows, LANES), jnp.float32)
 
     load.wait()
     for l in range(layers):
         rows_out[0, l : l + 1, :] = x[l, 0:1, LANES : LANES + cols]
         rows_out[1, l : l + 1, :] = x[l, rows - 1 : rows, LANES : LANES + cols]
 
-    def part_at(s, place):
-        return lax.rem(place // Q + jnp.where(s == 0, 2, jnp.where(s == 1, 1, jnp.where(s == 2, 3, 0))), PARTS)
-
-    def rows_copy(side, s):
-        at = pl.ds(pl.multiple_of(part_at(s, z) * width, width), width)
-        return pltpu.make_async_remote_copy(
-            src_ref=rows_out.at[1 - side, :, at],
-            dst_ref=rows_in.at[side, :, at],
-            send_sem=rows_ss.at[side, s],
-            recv_sem=rows_rs.at[side, s],
-            device_id=(me, down if side == 0 else up),
-            device_id_type=MESH,
-        )
-
-    def depth_copy(side, s, place, gx):
-        start = pl.multiple_of(part_at(s, place) * width, width)
-        return pltpu.make_async_remote_copy(
-            src_ref=x.at[layers - 1 if side == 0 else 0, :, pl.ds(pl.multiple_of(start + LANES, LANES), width)],
-            dst_ref=depth_in.at[side, :, pl.ds(start, width)],
-            send_sem=depth_ss.at[side, s],
-            recv_sem=depth_rs.at[side, s],
-            device_id=(gx, my),
-            device_id_type=MESH,
-        )
-
-    def p1_copy(s, k):
-        to = lax.rem(y + k, Q)
-        return pltpu.make_async_remote_copy(
-            src_ref=p1s.at[s, to],
-            dst_ref=p1r.at[s, k],
-            send_sem=p1_ss.at[s, k],
-            recv_sem=p1_rs.at[s, k],
-            device_id=(z * Q + to, my),
-            device_id_type=MESH,
-        )
-
-    def p2_copy(to):
-        k = lax.rem(to + nz - z, nz)
-        return pltpu.make_async_remote_copy(
-            src_ref=p2s.at[to],
-            dst_ref=p2r.at[k],
-            send_sem=p2_ss.at[k],
-            recv_sem=p2_rs.at[k],
-            device_id=(to * Q + y, my),
-            device_id_type=MESH,
-        )
-
-    pl.semaphore_wait(barrier, 4 + (Q - 1) + (nz - 1))
-
-    def send_halos(s, _):
-        for side in range(2):
-            rows_copy(side, s).start()
+    pl.semaphore_wait(barrier, 4 + 2 + (nz - 1))
+
+    def send_depth(s):
         depth_copy(0, s, nxt // Q, nxt).start()
         depth_copy(1, s, prv // Q, prv).start()
-        return 0
-
-    lax.fori_loop(0, PARTS, send_halos, 0)
+
+    send_depth(0)
+    for side in range(2):
+        rows_copy(side).start()
+    send_depth(1)
 
     lane = lax.broadcasted_iota(jnp.int32, tile, 1)
     row = lax.broadcasted_iota(jnp.int32, tile, 0)
     lane_all = lax.broadcasted_iota(jnp.int32, (rows, LANES), 1)
-    lane_part = lax.broadcasted_iota(jnp.int32, (per, rows, LANES), 2)
     from_prv = jnp.where(me > 0, 1.0, 0.0).astype(jnp.float32)
     from_nxt = jnp.where(me < nx - 1, 1.0, 0.0).astype(jnp.float32)
     from_up = jnp.where(my > 0, 1.0, 0.0).astype(jnp.float32)
@@ -251,35 +269,56 @@
             for b in range(n_lane):
                 cut = slice(LANES * b, LANES * b + LANES)
                 owned = regroup([v[:, cut] for v in colour + [opaque]], lane_all)
-                for j in range(Q):
-                    p1s[s, j, i * n_lane + b] = owned[j]
+                for place, j in enumerate((0, 3, 1, 2)):
+                    p1s[s, place, i * n_lane + b] = owned[j]
             return 0
 
         lax.fori_loop(0, width // SUB, one, 0)
+
+    def ordered(mine, theirs, mine_first):
+        return jnp.where(mine_first, mine, theirs), jnp.where(mine_first, theirs, mine)
 
     def step(s, _):
         @pl.when(s < PARTS)
         def _():
             part = part_at(s, z)
+
+            @pl.when(s + 2 < PARTS)
+            def _():
+                send_depth(s + 2)
+
             emit(part)
+
+            @pl.when(s == 0)
+            def _():
+                for side in range(2):
+                    rows_copy(side).wait_recv()
+
             for side in range(2):
-                rows_copy(side, s).wait_recv()
                 depth_copy(side, s, z, (nxt, prv)[side]).wait_recv()
             march(s, part)
-            for k in (2, 1, 3):
-                p1_copy(s, k).start()
-
-        @pl.when(s > 0)
+            p1_copy(s).start()
+
+        @pl.when((s >= 2) & (s < PARTS + 2))
         def _():
-            t = s - 1
+            t = s - 2
+            p1_copy(t).wait_recv()
+            flat = (2 * per * rows, LANES)
+            mine, theirs = p1s[t, pl.ds(kept, 2)].reshape(flat), p1r[t].reshape(flat)
+            front, back = ordered(mine, theirs, partner > y)
+            lane_flat = lax.broadcasted_iota(jnp.int32, flat, 1)
+            pair[t] = over(front, back, lane_flat).reshape(2, per, rows, LANES)
+            r1_copy(t).start()
+
+        @pl.when(s >= 4)
+        def _():
+            t = s - 4
             part = part_at(t, z)
-            p1r[t, 0] = p1s[t, y]
-            for k in range(1, Q):
-                p1_copy(t, k).wait_recv()
-            total = p1r[t, lax.rem(y + 1, Q)]
-            for j in range(Q - 2, -1, -1):
-                total = over(p1r[t, lax.rem(y + Q - j, Q)].reshape(per * rows, LANES), total.reshape(per * rows, LANES), lane_flat)
-            total = total.reshape(per, rows, LANES)
+            r1_copy(t).wait_recv()
+            flat = (per * rows, LANES)
+            front, back = ordered(pair[t, own].reshape(flat), r1r[t].reshape(flat), mirror > y)
+            lane_flat = lax.broadcasted_iota(jnp.int32, flat, 1)
+            total = over(front, back, lane_flat).reshape(per, rows, LANES)
             for b in range(per):
                 to = part * per + b
                 p2s[to] = total[b]
@@ -290,39 +329,33 @@
 
         return 0
 
-    lane_flat = lax.broadcasted_iota(jnp.int32, (per * rows, LANES), 1)
-    lax.fori_loop(0, PARTS + 1, step, 0)
+    lax.fori_loop(0, PARTS + 4, step, 0)
 
     p2r[0] = p2s[z]
 
+    for side in range(2):
+        rows_copy(side).wait_send()
+
+    def finish(s, _):
+        for side in range(2):
+            depth_copy(side, s, z, (nxt, prv)[side]).wait_send()
+        p1_copy(s).wait_send()
+        r1_copy(s).wait_send()
+        return 0
+
+    lax.fori_loop(0, PARTS, finish, 0)
+
     def wait_p2(k, _):
-        p2_copy(lax.rem(z + k, nz)).wait_recv()
+        p2_copy(lax.rem(z + k, nz)).wait()
         return 0
 
     lax.fori_loop(1, nz, wait_p2, 0)
 
-    def behind_all(i, total):
-        return over(p2r[lax.rem(z + 1 + i, nz)], total, lane_all)
-
-    total = lax.fori_loop(1, nz, behind_all, p2r[lax.rem(z + 1, nz)])
+    total = p2r[lax.rem(z + 1, nz)]
+    for i in range(1, nz):
+        total = over(p2r[lax.rem(z + 1 + i, nz)], total, lane_all)
     for c in range(4):
         out[c] = total[:, G * c : G * c + G]
-
-    def finish_halos(s, _):
-        for side in range(2):
-            rows_copy(side, s).wait_send()
-            depth_copy(side, s, z, (nxt, prv)[side]).wait_send()
-        for k in range(1, Q):
-            p1_copy(s, k).wait_send()
-        return 0
-
-    lax.fori_loop(0, PARTS, finish_halos, 0)
-
-    def finish_p2(k, _):
-        p2_copy(lax.rem(z + k, nz)).wait_send()
-        return 0
-
-    lax.fori_loop(1, nz, finish_p2, 0)
 
 
 def local(nx, ny, density, centers, widths, weights, colors, light):
@@ -331,14 +364,15 @@
     width = cols // PARTS
     per = width // LANES
     dma = pltpu.SemaphoreType.DMA
-    smem = pl.BlockSpec(memory_space=pltpu.SMEM)
+    hbm = pl.BlockSpec(memory_space=pltpu.HBM)
     f32 = jnp.float32
     return pl.pallas_call(
         functools.partial(kernel, nx, ny, 1.5 / (layers * nx)),
         out_shape=jax.ShapeDtypeStruct((4, rows, cols // nx), f32),
-        in_specs=[pl.BlockSpec(memory_space=pl.ANY)] + [smem] * 5,
+        in_specs=[hbm] * 6,
         out_specs=pl.BlockSpec(memory_space=pltpu.VMEM),
-        scratch_shapes=[
+        scratch_shapes=[pltpu.SMEM(given.shape, f32) for given in (centers, widths, weights, colors, light)]
+        + [
             pltpu.VMEM((layers, rows, cols + 2 * LANES), f32),
             pltpu.VMEM((2, layers, cols), f32),
             pltpu.VMEM((2, layers, cols), f32),
@@ -346,16 +380,21 @@
             pltpu.VMEM((6 * bumps + 3, 8, LANES), f32),
             pltpu.VMEM((4, layers, rows, width), f32),
             pltpu.VMEM((PARTS, Q, per, rows, LANES), f32),
-            pltpu.VMEM((PARTS, Q, per, rows, LANES), f32),
+            pltpu.VMEM((PARTS, 2, per, rows, LANES), f32),
+            pltpu.VMEM((PARTS, 2, per, rows, LANES), f32),
+            pltpu.VMEM((PARTS, per, rows, LANES), f32),
             pltpu.VMEM((nz, rows, LANES), f32),
             pltpu.VMEM((nz, rows, LANES), f32),
             dma,
+            dma((5,)),
+            dma((2,)),
+            dma((2,)),
             dma((2, PARTS)),
             dma((2, PARTS)),
-            dma((2, PARTS)),
-            dma((2, PARTS)),
-            dma((PARTS, Q)),
-            dma((PARTS, Q)),
+            dma((PARTS,)),
+            dma((PARTS,)),
+            dma((PARTS,)),
+            dma((PARTS,)),
             dma((nz,)),
             dma((nz,)),
         ],
@@ -365,7 +404,7 @@
         cost_estimate=pl.CostEstimate(
             flops=130 * density.size, bytes_accessed=4 * density.size, transcendentals=9 * density.size
         ),
-    )(density, centers, widths, weights, colors, light)
+    )(*(pltpu.with_memory_space_constraint(v, pltpu.HBM) for v in (density, centers, widths, weights, colors, light)))
 
 
 def solution(mesh):

time: 49.5 us -> 46.5 us (0.939)
  the two profiles are of different devices: /device:TPU:6 before, /device:TPU:36 now
where the time goes in v2:
time: 46.5 us; the launch traced here: 46.4 us
  Pallas kernels  45.7 us (98%)
  local copies, waits for them, and re-layouts  0.62 us (1%)
    pallas_call x1, Pallas kernels, local(): pl.pallas_call(functools.partial(kernel, nx, ny, 1.5 / (layers * nx)), ou...  45.7 us

profile of v2, /device:TPU:36, one launch (start us, length us, event | category | flops | bytes accessed | tf_op | source)
XLA Modules:
  0.0 46.4 jit_solution(13825071068607632570)
XLA Ops:
  0.0 45.7 %shard_map.64 = f32[4,24,32]{2,1,0:T(8,128)S(1)} custom-call(f32[8,24,2048]{2,1,0:T(8,128)} %density.1, f32[8]{0:T(128)} %rest_0_.1, f32[8]{0:T(128)} %rest_1_.1, f32[8]{0:T(128)} %rest_2_.1, f32[3,8]{1,0:T(4,128)} %rest_3_.1, f32[3]{0:T(128)} %rest_4_.1), custom_call_target="tpu_custom_call" | custom-call | flops 51118080 | bytes 1572864 | tf_op jit(solution)/shard_map/pallas_call | solution.py:369
  45.7 0.6 %copy.8 = f32[4,24,32]{2,1,0:T(8,128)} copy(f32[4,24,32]{2,1,0:T(8,128)S(1)} %shard_map.64) | data formatting | bytes 24576

commit v3 on v2

--- a/solution.py
+++ b/solution.py
@@ -13,6 +13,7 @@
 Q = 4
 G = LANES // Q
 PARTS = 8
+LEAD = 3
 SUB = 256
 
 
@@ -57,8 +58,8 @@
 ):
     given, rest = rest[:5], rest[5:]
     out, centers, widths, weights, colors, light = rest[:6]
-    x, rows_out, rows_in, depth_in, prm, emi, p1s, p1r, pair, r1r, p2s, p2r = rest[6:18]
-    x_sem, given_sem, rows_ss, rows_rs, depth_ss, depth_rs, p1_ss, p1_rs, r1_ss, r1_rs, p2_ss, p2_rs = rest[18:]
+    x, rows_out, rows_in, depth_in, prm, emi, p1s, p1r, lastr, p2s, p2r = rest[6:17]
+    x_sem, given_sem, rows_ss, rows_rs, depth_ss, depth_rs, p1_ss, p1_rs, last_ss, last_rs, p2_ss, p2_rs = rest[17:]
     layers, rows, cols = density.shape
     nz = nx // Q
     bumps = centers.shape[0]
@@ -66,9 +67,7 @@
     per = width // LANES
     me, my = lax.axis_index("gx"), lax.axis_index("gy")
     z, y = me // Q, lax.rem(me, Q)
-    partner, mirror = y + 1 - 2 * lax.rem(y, 2), Q - 1 - y
-    kept = jnp.where((y == 0) | (y == Q - 1), 0, 2)
-    own = y // 2
+    first_z, in_group = z // per * per, lax.rem(z, per)
     nxt, prv = lax.rem(me + 1, nx), lax.rem(me + nx - 1, nx)
     down, up = lax.rem(my + 1, ny), lax.rem(my + ny - 1, ny)
 
@@ -95,9 +94,10 @@
         greet(lax.rem(z + k, nz) * Q + y, my)
         return 0
 
-    greet(z * Q + partner, my)
-    greet(z * Q + mirror, my)
     lax.fori_loop(1, nz, greet_z, 0)
+    for k in range(1, Q):
+        for g in range(per):
+            greet((first_z + lax.rem(in_group + g, per)) * Q + lax.rem(y + k, Q), my)
     x[:, :, :LANES] = jnp.zeros((layers, rows, LANES), jnp.float32)
     x[:, :, LANES + cols :] = jnp.zeros((layers, rows, LANES), jnp.float32)
 
@@ -126,28 +126,30 @@
             device_id_type=MESH,
         )
 
-    def p1_copy(s):
+    def p1_copy(s, k):
+        to = lax.rem(y + k, Q)
         return pltpu.make_async_remote_copy(
-            src_ref=p1s.at[s, pl.ds(2 - kept, 2)],
-            dst_ref=p1r.at[s],
-            send_sem=p1_ss.at[s],
-            recv_sem=p1_rs.at[s],
-            device_id=(z * Q + partner, my),
+            src_ref=p1s.at[s, to],
+            dst_ref=p1r.at[s, k],
+            send_sem=p1_ss.at[s, k],
+            recv_sem=p1_rs.at[s, k],
+            device_id=(z * Q + to, my),
             device_id_type=MESH,
         )
 
-    def r1_copy(s):
+    def last_copy(g, k):
+        at, to = lax.rem(in_group + g, per), lax.rem(y + k, Q)
         return pltpu.make_async_remote_copy(
-            src_ref=pair.at[s, 1 - own],
-            dst_ref=r1r.at[s],
-            send_sem=r1_ss.at[s],
-            recv_sem=r1_rs.at[s],
-            device_id=(z * Q + mirror, my),
+            src_ref=p1s.at[PARTS - 1, to, at],
+            dst_ref=lastr.at[g, k],
+            send_sem=last_ss.at[g, k],
+            recv_sem=last_rs.at[g, k],
+            device_id=((first_z + at) * Q + to, my),
             device_id_type=MESH,
         )
 
-    def p2_copy(to):
-        k = lax.rem(to + nz - z, nz)
+    def p2_copy(k):
+        to = lax.rem(z + k, nz)
         return pltpu.make_async_remote_copy(
             src_ref=p2s.at[to],
             dst_ref=p2r.at[k],
@@ -176,17 +178,6 @@
         rows_out[0, l : l + 1, :] = x[l, 0:1, LANES : LANES + cols]
         rows_out[1, l : l + 1, :] = x[l, rows - 1 : rows, LANES : LANES + cols]
 
-    pl.semaphore_wait(barrier, 4 + 2 + (nz - 1))
-
-    def send_depth(s):
-        depth_copy(0, s, nxt // Q, nxt).start()
-        depth_copy(1, s, prv // Q, prv).start()
-
-    send_depth(0)
-    for side in range(2):
-        rows_copy(side).start()
-    send_depth(1)
-
     lane = lax.broadcasted_iota(jnp.int32, tile, 1)
     row = lax.broadcasted_iota(jnp.int32, tile, 0)
     lane_all = lax.broadcasted_iota(jnp.int32, (rows, LANES), 1)
@@ -199,7 +190,9 @@
     def wide(i):
         return jnp.tile(prm[i], reps)
 
-    def emit(part):
+    def emit(s):
+        part = part_at(s, z)
+
         def one(i, _):
             l, start = lax.rem(i, layers), (i // layers) * SUB
             cells = x[l, :, pl.ds(pl.multiple_of(part * width + start + LANES, LANES), SUB)]
@@ -213,7 +206,7 @@
             opacity = t * (1.0 - t * (0.5 - t * (1.0 / 6.0 - t * (1.0 / 24.0))))
             at = pl.ds(pl.multiple_of(start, SUB), SUB)
             for c, v in enumerate([opacity] + sums[1:]):
-                emi[c, l, :, at] = v
+                emi[s, c, l, :, at] = v
             return 0
 
         lax.fori_loop(0, layers * (width // SUB), one, 0)
@@ -226,7 +219,9 @@
     def joined(tiles):
         return jnp.concatenate([jnp.concatenate(line, 1) for line in tiles], 0)
 
-    def march(s, part):
+    def march(s):
+        part = part_at(s, z)
+
         def one(i, _):
             at = pl.multiple_of(part * width + i * SUB, SUB)
             here = pl.ds(pl.multiple_of(i * SUB, SUB), SUB)
@@ -261,77 +256,85 @@
                     + hz * (joined(ahead) - joined(behind))
                 )
                 shading = 0.625 + 0.375 * jnp.tanh(facing)
-                seen = clear * emi[0, l, :, here]
+                seen = clear * emi[s, 0, l, :, here]
                 clear, opaque = clear - seen, opaque + seen
                 lit = seen * shading
-                colour = [colour[c] + lit * emi[c + 1, l, :, here] for c in range(3)]
+                colour = [colour[c] + lit * emi[s, c + 1, l, :, here] for c in range(3)]
                 before, cells = cells, after
             for b in range(n_lane):
                 cut = slice(LANES * b, LANES * b + LANES)
                 owned = regroup([v[:, cut] for v in colour + [opaque]], lane_all)
-                for place, j in enumerate((0, 3, 1, 2)):
-                    p1s[s, place, i * n_lane + b] = owned[j]
+                for j in range(Q):
+                    p1s[s, j, i * n_lane + b] = owned[j]
             return 0
 
         lax.fori_loop(0, width // SUB, one, 0)
 
-    def ordered(mine, theirs, mine_first):
-        return jnp.where(mine_first, mine, theirs), jnp.where(mine_first, theirs, mine)
+    emit(0)
+    pl.semaphore_wait(barrier, 4 + (nz - 1) + per * (Q - 1))
+
+    def send_depth(s):
+        depth_copy(0, s, nxt // Q, nxt).start()
+        depth_copy(1, s, prv // Q, prv).start()
+
+    send_depth(0)
+    for side in range(2):
+        rows_copy(side).start()
+    for s in range(1, LEAD):
+        send_depth(s)
+    for s in range(1, LEAD):
+        emit(s)
+    for side in range(2):
+        rows_copy(side).wait_recv()
+
 
     def step(s, _):
+        @pl.when((s >= LEAD) & (s < PARTS))
+        def _():
+            emit(s)
+
         @pl.when(s < PARTS)
         def _():
-            part = part_at(s, z)
-
-            @pl.when(s + 2 < PARTS)
+            @pl.when(s + LEAD < PARTS)
             def _():
-                send_depth(s + 2)
-
-            emit(part)
-
-            @pl.when(s == 0)
-            def _():
-                for side in range(2):
-                    rows_copy(side).wait_recv()
+                send_depth(s + LEAD)
 
             for side in range(2):
                 depth_copy(side, s, z, (nxt, prv)[side]).wait_recv()
-            march(s, part)
-            p1_copy(s).start()
-
-        @pl.when((s >= 2) & (s < PARTS + 2))
+            march(s)
+
+        @pl.when(s < PARTS - 1)
+        def _():
+            for k in (2, 1, 3):
+                p1_copy(s, k).start()
+
+        @pl.when(s == PARTS - 1)
+        def _():
+            for g in range(per):
+                for k in range(Q):
+                    if (g, k) != (0, 0):
+                        last_copy(g, k).start()
+
+        @pl.when(s >= 2)
         def _():
             t = s - 2
-            p1_copy(t).wait_recv()
-            flat = (2 * per * rows, LANES)
-            mine, theirs = p1s[t, pl.ds(kept, 2)].reshape(flat), p1r[t].reshape(flat)
-            front, back = ordered(mine, theirs, partner > y)
+            first = part_at(t, z) * per
+            p1r[t, 0] = p1s[t, y]
+            for k in range(1, Q):
+                p1_copy(t, k).wait_recv()
+            flat = (per * rows, LANES)
             lane_flat = lax.broadcasted_iota(jnp.int32, flat, 1)
-            pair[t] = over(front, back, lane_flat).reshape(2, per, rows, LANES)
-            r1_copy(t).start()
-
-        @pl.when(s >= 4)
-        def _():
-            t = s - 4
-            part = part_at(t, z)
-            r1_copy(t).wait_recv()
-            flat = (per * rows, LANES)
-            front, back = ordered(pair[t, own].reshape(flat), r1r[t].reshape(flat), mirror > y)
-            lane_flat = lax.broadcasted_iota(jnp.int32, flat, 1)
-            total = over(front, back, lane_flat).reshape(per, rows, LANES)
+            total = p1r[t, lax.rem(y + 1, Q)].reshape(flat)
+            for j in range(Q - 2, -1, -1):
+                total = over(p1r[t, lax.rem(y + Q - j, Q)].reshape(flat), total, lane_flat)
+            total = total.reshape(per, rows, LANES)
             for b in range(per):
-                to = part * per + b
-                p2s[to] = total[b]
-
-                @pl.when(to != z)
-                def _():
-                    p2_copy(to).start()
+                p2s[first + b] = total[b]
+                p2_copy(lax.rem(first + b + nz - z, nz)).start()
 
         return 0
 
-    lax.fori_loop(0, PARTS + 4, step, 0)
-
-    p2r[0] = p2s[z]
+    lax.fori_loop(0, PARTS + 1, step, 0)
 
     for side in range(2):
         rows_copy(side).wait_send()
@@ -339,17 +342,35 @@
     def finish(s, _):
         for side in range(2):
             depth_copy(side, s, z, (nxt, prv)[side]).wait_send()
-        p1_copy(s).wait_send()
-        r1_copy(s).wait_send()
+
+        @pl.when(s < PARTS - 1)
+        def _():
+            for k in range(1, Q):
+                p1_copy(s, k).wait_send()
+
         return 0
 
     lax.fori_loop(0, PARTS, finish, 0)
 
-    def wait_p2(k, _):
-        p2_copy(lax.rem(z + k, nz)).wait()
+    lastr[0, 0] = p1s[PARTS - 1, y, in_group]
+    for g in range(per):
+        for k in range(Q):
+            if (g, k) != (0, 0):
+                last_copy(g, k).wait()
+    for g in range(per):
+        near = lax.rem(in_group + per - g, per)
+        total = lastr[near, lax.rem(y + 1, Q)]
+        for j in range(Q - 2, -1, -1):
+            total = over(lastr[near, lax.rem(y + Q - j, Q)], total, lane_all)
+        p2r[lax.rem(z + nz - (first_z + g), nz)] = total
+
+    def finish_p2(i, _):
+        other = lax.rem(first_z + i, nz)
+        p2_copy(lax.rem(other + nz - z, nz)).wait_send()
+        p2_copy(lax.rem(z + nz - other, nz)).wait_recv()
         return 0
 
-    lax.fori_loop(1, nz, wait_p2, 0)
+    lax.fori_loop(per, nz, finish_p2, 0)
 
     total = p2r[lax.rem(z + 1, nz)]
     for i in range(1, nz):
@@ -378,11 +399,10 @@
             pltpu.VMEM((2, layers, cols), f32),
             pltpu.VMEM((2, rows, cols), f32),
             pltpu.VMEM((6 * bumps + 3, 8, LANES), f32),
-            pltpu.VMEM((4, layers, rows, width), f32),
+            pltpu.VMEM((PARTS, 4, layers, rows, width), f32),
             pltpu.VMEM((PARTS, Q, per, rows, LANES), f32),
-            pltpu.VMEM((PARTS, 2, per, rows, LANES), f32),
-            pltpu.VMEM((PARTS, 2, per, rows, LANES), f32),
-            pltpu.VMEM((PARTS, per, rows, LANES), f32),
+            pltpu.VMEM((PARTS - 1, Q, per, rows, LANES), f32),
+            pltpu.VMEM((per, Q, rows, LANES), f32),
             pltpu.VMEM((nz, rows, LANES), f32),
             pltpu.VMEM((nz, rows, LANES), f32),
             dma,
@@ -391,10 +411,10 @@
             dma((2,)),
             dma((2, PARTS)),
             dma((2, PARTS)),
-            dma((PARTS,)),
-            dma((PARTS,)),
-            dma((PARTS,)),
-            dma((PARTS,)),
+            dma((PARTS - 1, Q)),
+            dma((PARTS - 1, Q)),
+            dma((per, Q)),
+            dma((per, Q)),
             dma((nz,)),
             dma((nz,)),
         ],

time: 46.5 us -> 42.3 us (0.910)
  the two profiles are of different devices: /device:TPU:36 before, /device:TPU:6 now
where the time goes in v3:
time: 42.3 us; the launch traced here: 41.6 us
  Pallas kernels  40.9 us (97%)
  local copies, waits for them, and re-layouts  0.62 us (1%)
    pallas_call x1, Pallas kernels, local(): pl.pallas_call(functools.partial(kernel, nx, ny, 1.5 / (layers * nx)), ou...  40.9 us

profile of v3, /device:TPU:6, one launch (start us, length us, event | category | flops | bytes accessed | tf_op | source)
XLA Modules:
  0.0 41.6 jit_solution(8259683610289903511)
XLA Ops:
  0.0 40.9 %shard_map.64 = f32[4,24,32]{2,1,0:T(8,128)S(1)} custom-call(f32[8,24,2048]{2,1,0:T(8,128)} %density.1, f32[8]{0:T(128)} %rest_0_.1, f32[8]{0:T(128)} %rest_1_.1, f32[8]{0:T(128)} %rest_2_.1, f32[3,8]{1,0:T(4,128)} %rest_3_.1, f32[3]{0:T(128)} %rest_4_.1), custom_call_target="tpu_custom_call" | custom-call | flops 51118080 | bytes 1572864 | tf_op jit(solution)/shard_map/pallas_call | solution.py:390
  41.0 0.6 %copy.8 = f32[4,24,32]{2,1,0:T(8,128)} copy(f32[4,24,32]{2,1,0:T(8,128)S(1)} %shard_map.64) | data formatting | bytes 24576

commit v4 on v3

--- a/solution.py
+++ b/solution.py
@@ -13,8 +13,7 @@
 Q = 4
 G = LANES // Q
 PARTS = 8
-LEAD = 3
-SUB = 256
+LEAD = 2
 
 
 def roll_lanes(v, by):
@@ -23,12 +22,11 @@
 
 def shifted(tiles, by, edge, lane_or_row, axis):
     size = tiles[0].shape[axis]
-    rolled = [pltpu.roll(t, by % size, axis=axis) for t in tiles]
     if by > 0:
-        before = [edge] + rolled[:-1]
-        return [jnp.where(lane_or_row == 0, b, r) for b, r in zip(before, rolled)]
-    after = rolled[1:] + [edge]
-    return [jnp.where(lane_or_row == size - 1, a, r) for a, r in zip(after, rolled)]
+        ahead, at = [edge] + tiles[:-1], size - 1
+    else:
+        ahead, at = tiles[1:] + [edge], 0
+    return [pltpu.roll(jnp.where(lane_or_row == at, a, t), by % size, axis=axis) for a, t in zip(ahead, tiles)]
 
 
 def regroup(values, lane):
@@ -185,90 +183,97 @@
     from_nxt = jnp.where(me < nx - 1, 1.0, 0.0).astype(jnp.float32)
     from_up = jnp.where(my > 0, 1.0, 0.0).astype(jnp.float32)
     from_down = jnp.where(my < ny - 1, 1.0, 0.0).astype(jnp.float32)
-    reps = (rows // 8, SUB // LANES)
+    n_row = rows // 8
 
     def wide(i):
-        return jnp.tile(prm[i], reps)
+        return jnp.concatenate([prm[i]] * n_row, 0)
+
+    def split(v):
+        return [v[8 * r : 8 * r + 8] for r in range(n_row)]
+
+    def column_of(s, i):
+        return pl.multiple_of(part_at(s, z) * width + i * LANES, LANES)
+
+    def emit_layer(s, i, at, l):
+        cells = x[l, :, pl.ds(pl.multiple_of(at + LANES, LANES), LANES)]
+        sums = None
+        for k in range(bumps):
+            scaled = (cells - wide(6 * k)) * wide(6 * k + 1)
+            step = jnp.exp2(wide(6 * k + 2) - scaled * scaled)
+            terms = [step] + [step * wide(6 * k + 3 + c) for c in range(3)]
+            sums = terms if sums is None else [a + b for a, b in zip(sums, terms)]
+        t = sums[0]
+        opacity = t * (1.0 - t * (0.5 - t * (1.0 / 6.0 - t * (1.0 / 24.0))))
+        for c, v in enumerate([opacity] + sums[1:]):
+            emi[s, i, l, c] = v
+
+    def march_layer(s, i, at, l, state):
+        clear, opaque, colour = state
+        here = pl.ds(at, LANES)
+
+        def layer(n):
+            return x[n, :, pl.ds(pl.multiple_of(at + LANES, LANES), LANES)]
+
+        before = layer(l - 1) if l > 0 else depth_in[0, :, here] * from_prv
+        after = layer(l + 1) if l < layers - 1 else depth_in[1, :, here] * from_nxt
+        tiles = split(layer(l))
+        left = split(x[l, :, pl.ds(at, LANES)])
+        right = split(x[l, :, pl.ds(pl.multiple_of(at + 2 * LANES, LANES), LANES)])
+        over_row = jnp.broadcast_to(rows_in[0, l : l + 1, here], tile) * from_up
+        under_row = jnp.broadcast_to(rows_in[1, l : l + 1, here], tile) * from_down
+        behind = [shifted([t], 1, e, lane, 1)[0] for t, e in zip(tiles, left)]
+        ahead = [shifted([t], -1, e, lane, 1)[0] for t, e in zip(tiles, right)]
+        above = shifted(tiles, 1, over_row, row, 0)
+        below = shifted(tiles, -1, under_row, row, 0)
+        hx, hy, hz = (wide(6 * bumps + c) for c in range(3))
+        facing = (
+            hx * (after - before)
+            + hy * jnp.concatenate([b - a for a, b in zip(above, below)], 0)
+            + hz * jnp.concatenate([b - a for a, b in zip(behind, ahead)], 0)
+        )
+        shading = 0.625 + 0.375 * jnp.tanh(facing)
+        seen = clear * emi[s, i, l, 0]
+        lit = seen * shading
+        return clear - seen, opaque + seen, [colour[c] + lit * emi[s, i, l, c + 1] for c in range(3)]
+
+    def march_end(s, i, state):
+        owned = regroup(state[2] + [state[1]], lane_all)
+        for j in range(Q):
+            p1s[s, j, i] = owned[j]
+
+    zero = jnp.zeros((rows, LANES), jnp.float32)
+    fresh = (jnp.ones((rows, LANES), jnp.float32), zero, [zero] * 3)
 
     def emit(s):
-        part = part_at(s, z)
-
+        def one(n, _):
+            i, l = lax.rem(n, per), n // per * 2
+            at = column_of(s, i)
+            emit_layer(s, i, at, l)
+            emit_layer(s, i, at, l + 1)
+            return 0
+
+        lax.fori_loop(0, per * layers // 2, one, 0)
+
+    def march(s):
         def one(i, _):
-            l, start = lax.rem(i, layers), (i // layers) * SUB
-            cells = x[l, :, pl.ds(pl.multiple_of(part * width + start + LANES, LANES), SUB)]
-            sums = None
-            for k in range(bumps):
-                scaled = (cells - wide(6 * k)) * wide(6 * k + 1)
-                step = jnp.exp2(wide(6 * k + 2) - scaled * scaled)
-                terms = [step] + [step * wide(6 * k + 3 + c) for c in range(3)]
-                sums = terms if sums is None else [a + b for a, b in zip(sums, terms)]
-            t = sums[0]
-            opacity = t * (1.0 - t * (0.5 - t * (1.0 / 6.0 - t * (1.0 / 24.0))))
-            at = pl.ds(pl.multiple_of(start, SUB), SUB)
-            for c, v in enumerate([opacity] + sums[1:]):
-                emi[s, c, l, :, at] = v
+            at, state = column_of(s, i), fresh
+            for l in range(layers):
+                state = march_layer(s, i, at, l, state)
+            march_end(s, i, state)
             return 0
 
-        lax.fori_loop(0, layers * (width // SUB), one, 0)
-
-    n_lane, n_row = SUB // LANES, rows // 8
-
-    def grid_of(v):
-        return [[v[8 * r : 8 * r + 8, LANES * c : LANES * c + LANES] for c in range(v.shape[1] // LANES)] for r in range(v.shape[0] // 8)]
-
-    def joined(tiles):
-        return jnp.concatenate([jnp.concatenate(line, 1) for line in tiles], 0)
-
-    def march(s):
-        part = part_at(s, z)
-
+        lax.fori_loop(0, per, one, 0)
+
+    def emit_and_march(e, s):
         def one(i, _):
-            at = pl.multiple_of(part * width + i * SUB, SUB)
-            here = pl.ds(pl.multiple_of(i * SUB, SUB), SUB)
-            hx, hy, hz = (wide(6 * bumps + c) for c in range(3))
-            clear = jnp.ones((rows, SUB), jnp.float32)
-            opaque = jnp.zeros((rows, SUB), jnp.float32)
-            colour = [jnp.zeros((rows, SUB), jnp.float32) for c in range(3)]
-
-            def layer(l):
-                return x[l, :, pl.ds(pl.multiple_of(at + LANES, LANES), SUB)]
-
-            before, cells = depth_in[0, :, pl.ds(at, SUB)] * from_prv, layer(0)
+            emit_at, at, state = column_of(e, i), column_of(s, i), fresh
             for l in range(layers):
-                after = layer(l + 1) if l < layers - 1 else depth_in[1, :, pl.ds(at, SUB)] * from_nxt
-                tiles = grid_of(cells)
-                left = grid_of(x[l, :, pl.ds(at, LANES)])
-                right = grid_of(x[l, :, pl.ds(pl.multiple_of(at + LANES + SUB, LANES), LANES)])
-                behind = [shifted(tiles[r], 1, roll_lanes(left[r][0], 1), lane, 1) for r in range(n_row)]
-                ahead = [shifted(tiles[r], -1, roll_lanes(right[r][0], -1), lane, 1) for r in range(n_row)]
-                over_row = jnp.broadcast_to(rows_in[0, l : l + 1, pl.ds(at, SUB)], (8, SUB)) * from_up
-                under_row = jnp.broadcast_to(rows_in[1, l : l + 1, pl.ds(at, SUB)], (8, SUB)) * from_down
-                above, below = [], []
-                for c in range(n_lane):
-                    column = [tiles[r][c] for r in range(n_row)]
-                    above.append(shifted(column, 1, over_row[:, LANES * c : LANES * c + LANES], row, 0))
-                    below.append(shifted(column, -1, under_row[:, LANES * c : LANES * c + LANES], row, 0))
-                above = [[above[c][r] for c in range(n_lane)] for r in range(n_row)]
-                below = [[below[c][r] for c in range(n_lane)] for r in range(n_row)]
-                facing = (
-                    hx * (after - before)
-                    + hy * (joined(below) - joined(above))
-                    + hz * (joined(ahead) - joined(behind))
-                )
-                shading = 0.625 + 0.375 * jnp.tanh(facing)
-                seen = clear * emi[s, 0, l, :, here]
-                clear, opaque = clear - seen, opaque + seen
-                lit = seen * shading
-                colour = [colour[c] + lit * emi[s, c + 1, l, :, here] for c in range(3)]
-                before, cells = cells, after
-            for b in range(n_lane):
-                cut = slice(LANES * b, LANES * b + LANES)
-                owned = regroup([v[:, cut] for v in colour + [opaque]], lane_all)
-                for j in range(Q):
-                    p1s[s, j, i * n_lane + b] = owned[j]
+                emit_layer(e, i, emit_at, l)
+                state = march_layer(s, i, at, l, state)
+            march_end(s, i, state)
             return 0
 
-        lax.fori_loop(0, width // SUB, one, 0)
+        lax.fori_loop(0, per, one, 0)
 
     emit(0)
     pl.semaphore_wait(barrier, 4 + (nz - 1) + per * (Q - 1))
@@ -289,18 +294,18 @@
 
 
     def step(s, _):
-        @pl.when((s >= LEAD) & (s < PARTS))
-        def _():
-            emit(s)
-
         @pl.when(s < PARTS)
         def _():
-            @pl.when(s + LEAD < PARTS)
-            def _():
-                send_depth(s + LEAD)
-
             for side in range(2):
                 depth_copy(side, s, z, (nxt, prv)[side]).wait_recv()
+
+        @pl.when(s + LEAD < PARTS)
+        def _():
+            send_depth(s + LEAD)
+            emit_and_march(s + LEAD, s)
+
+        @pl.when((s + LEAD >= PARTS) & (s < PARTS))
+        def _():
             march(s)
 
         @pl.when(s < PARTS - 1)
@@ -399,7 +404,7 @@
             pltpu.VMEM((2, layers, cols), f32),
             pltpu.VMEM((2, rows, cols), f32),
             pltpu.VMEM((6 * bumps + 3, 8, LANES), f32),
-            pltpu.VMEM((PARTS, 4, layers, rows, width), f32),
+            pltpu.VMEM((PARTS, per, layers, 4, rows, LANES), f32),
             pltpu.VMEM((PARTS, Q, per, rows, LANES), f32),
             pltpu.VMEM((PARTS - 1, Q, per, rows, LANES), f32),
             pltpu.VMEM((per, Q, rows, LANES), f32),

time: 42.3 us -> 46.5 us (1.099)
  Pallas kernels: 40.9 us -> 45.3 us
    pallas_call x1, Pallas kernels: 40.9 us -> 45.3 us  [local(): pl.pallas_call(functools.partial(kernel, nx, ny, 1.5 / (layers * nx)), ou...]
where the time goes in v4:
time: 46.5 us; the launch traced here: 46 us
  Pallas kernels  45.3 us (97%)
  local copies, waits for them, and re-layouts  0.62 us (1%)
    pallas_call x1, Pallas kernels, local(): pl.pallas_call(functools.partial(kernel, nx, ny, 1.5 / (layers * nx)), ou...  45.3 us

profile of v4, /device:TPU:6, one launch (start us, length us, event | category | flops | bytes accessed | tf_op | source)
XLA Modules:
  0.0 46.0 jit_solution(14671071864580708052)
XLA Ops:
  0.0 45.3 %shard_map.64 = f32[4,24,32]{2,1,0:T(8,128)S(1)} custom-call(f32[8,24,2048]{2,1,0:T(8,128)} %density.1, f32[8]{0:T(128)} %rest_0_.1, f32[8]{0:T(128)} %rest_1_.1, f32[8]{0:T(128)} %rest_2_.1, f32[3,8]{1,0:T(4,128)} %rest_3_.1, f32[3]{0:T(128)} %rest_4_.1), custom_call_target="tpu_custom_call" | custom-call | flops 51118080 | bytes 1572864 | tf_op jit(solution)/shard_map/pallas_call | solution.py:395
  45.4 0.6 %copy.8 = f32[4,24,32]{2,1,0:T(8,128)} copy(f32[4,24,32]{2,1,0:T(8,128)S(1)} %shard_map.64) | data formatting | bytes 24576

commit v5 on v4

--- a/solution.py
+++ b/solution.py
@@ -289,6 +289,12 @@
         send_depth(s)
     for s in range(1, LEAD):
         emit(s)
+
+    def send_more(s, _):
+        send_depth(s)
+        return 0
+
+    lax.fori_loop(LEAD, PARTS, send_more, 0)
     for side in range(2):
         rows_copy(side).wait_recv()
 
@@ -301,7 +307,6 @@
 
         @pl.when(s + LEAD < PARTS)
         def _():
-            send_depth(s + LEAD)
             emit_and_march(s + LEAD, s)
 
         @pl.when((s + LEAD >= PARTS) & (s < PARTS))

time: 46.5 us -> 41.1 us (0.88)
  Pallas kernels: 45.3 us -> 40.4 us
    pallas_call x1, Pallas kernels: 45.3 us -> 40.4 us  [local(): pl.pallas_call(functools.partial(kernel, nx, ny, 1.5 / (layers * nx)), ou...]
where the time goes in v5:
time: 41.1 us; the launch traced here: 41 us
  Pallas kernels  40.4 us (98%)
  local copies, waits for them, and re-layouts  0.62 us (2%)
    pallas_call x1, Pallas kernels, local(): pl.pallas_call(functools.partial(kernel, nx, ny, 1.5 / (layers * nx)), ou...  40.4 us

profile of v5, /device:TPU:6, one launch (start us, length us, event | category | flops | bytes accessed | tf_op | source)
XLA Modules:
  0.0 41.0 jit_solution(12553703597061414403)
XLA Ops:
  0.0 40.4 %shard_map.64 = f32[4,24,32]{2,1,0:T(8,128)S(1)} custom-call(f32[8,24,2048]{2,1,0:T(8,128)} %density.1, f32[8]{0:T(128)} %rest_0_.1, f32[8]{0:T(128)} %rest_1_.1, f32[8]{0:T(128)} %rest_2_.1, f32[3,8]{1,0:T(4,128)} %rest_3_.1, f32[3]{0:T(128)} %rest_4_.1), custom_call_target="tpu_custom_call" | custom-call | flops 51118080 | bytes 1572864 | tf_op jit(solution)/shard_map/pallas_call | solution.py:400
  40.4 0.6 %copy.8 = f32[4,24,32]{2,1,0:T(8,128)} copy(f32[4,24,32]{2,1,0:T(8,128)S(1)} %shard_map.64) | data formatting | bytes 24576

commit v6 on v5

--- a/solution.py
+++ b/solution.py
@@ -14,6 +14,7 @@
 G = LANES // Q
 PARTS = 8
 LEAD = 2
+PASSED = 5
 
 
 def roll_lanes(v, by):
@@ -56,8 +57,8 @@
 ):
     given, rest = rest[:5], rest[5:]
     out, centers, widths, weights, colors, light = rest[:6]
-    x, rows_out, rows_in, depth_in, prm, emi, p1s, p1r, lastr, p2s, p2r = rest[6:17]
-    x_sem, given_sem, rows_ss, rows_rs, depth_ss, depth_rs, p1_ss, p1_rs, last_ss, last_rs, p2_ss, p2_rs = rest[17:]
+    x, rows_out, rows_in, depth_in, prm, emi, p1s, p1r, passed, lastr, p2s, p2r = rest[6:18]
+    x_sem, given_sem, rows_ss, rows_rs, depth_ss, depth_rs, p1_ss, p1_rs, pass_ss, pass_rs, last_ss, last_rs, p2_ss, p2_rs = rest[18:]
     layers, rows, cols = density.shape
     nz = nx // Q
     bumps = centers.shape[0]
@@ -132,6 +133,27 @@
             send_sem=p1_ss.at[s, k],
             recv_sem=p1_rs.at[s, k],
             device_id=(z * Q + to, my),
+            device_id_type=MESH,
+        )
+
+    def far_copy(s):
+        to = lax.rem(y + 2, Q)
+        return pltpu.make_async_remote_copy(
+            src_ref=p1s.at[s, to, 0],
+            dst_ref=p1r.at[s, 2, 0],
+            send_sem=p1_ss.at[s, 2],
+            recv_sem=p1_rs.at[s, 2],
+            device_id=(z * Q + to, my),
+            device_id_type=MESH,
+        )
+
+    def pass_copy(s, leg):
+        return pltpu.make_async_remote_copy(
+            src_ref=p1s.at[s, lax.rem(y + 2, Q), pl.ds(1, per - 1)] if leg == 0 else passed.at[s],
+            dst_ref=passed.at[s] if leg == 0 else p1r.at[s, 2, pl.ds(1, per - 1)],
+            send_sem=pass_ss.at[leg, s],
+            recv_sem=pass_rs.at[leg, s],
+            device_id=(z * Q + lax.rem(y + Q - 1, Q), my),
             device_id_type=MESH,
         )
 
@@ -254,8 +276,15 @@
 
         lax.fori_loop(0, per * layers // 2, one, 0)
 
+    def pass_on(s, i):
+        @pl.when((i == 1) & (s >= 2) & (s < PASSED + 2))
+        def _():
+            pass_copy(s - 2, 0).wait_recv()
+            pass_copy(s - 2, 1).start()
+
     def march(s):
         def one(i, _):
+            pass_on(s, i)
             at, state = column_of(s, i), fresh
             for l in range(layers):
                 state = march_layer(s, i, at, l, state)
@@ -266,6 +295,7 @@
 
     def emit_and_march(e, s):
         def one(i, _):
+            pass_on(s, i)
             emit_at, at, state = column_of(e, i), column_of(s, i), fresh
             for l in range(layers):
                 emit_layer(e, i, emit_at, l)
@@ -315,7 +345,16 @@
 
         @pl.when(s < PARTS - 1)
         def _():
-            for k in (2, 1, 3):
+            @pl.when(s < PASSED)
+            def _():
+                pass_copy(s, 0).start()
+                far_copy(s).start()
+
+            @pl.when(s >= PASSED)
+            def _():
+                p1_copy(s, 2).start()
+
+            for k in (1, 3):
                 p1_copy(s, k).start()
 
         @pl.when(s == PARTS - 1)
@@ -325,13 +364,23 @@
                     if (g, k) != (0, 0):
                         last_copy(g, k).start()
 
-        @pl.when(s >= 2)
-        def _():
-            t = s - 2
+        @pl.when(s >= 3)
+        def _():
+            t = s - 3
             first = part_at(t, z) * per
             p1r[t, 0] = p1s[t, y]
-            for k in range(1, Q):
+            for k in (1, 3):
                 p1_copy(t, k).wait_recv()
+
+            @pl.when(t < PASSED)
+            def _():
+                far_copy(t).wait_recv()
+                pass_copy(t, 1).wait_recv()
+
+            @pl.when(t >= PASSED)
+            def _():
+                p1_copy(t, 2).wait_recv()
+
             flat = (per * rows, LANES)
             lane_flat = lax.broadcasted_iota(jnp.int32, flat, 1)
             total = p1r[t, lax.rem(y + 1, Q)].reshape(flat)
@@ -344,7 +393,7 @@
 
         return 0
 
-    lax.fori_loop(0, PARTS + 1, step, 0)
+    lax.fori_loop(0, PARTS + 2, step, 0)
 
     for side in range(2):
         rows_copy(side).wait_send()
@@ -355,8 +404,18 @@
 
         @pl.when(s < PARTS - 1)
         def _():
-            for k in range(1, Q):
+            for k in (1, 3):
                 p1_copy(s, k).wait_send()
+
+            @pl.when(s < PASSED)
+            def _():
+                far_copy(s).wait_send()
+                for leg in range(2):
+                    pass_copy(s, leg).wait_send()
+
+            @pl.when(s >= PASSED)
+            def _():
+                p1_copy(s, 2).wait_send()
 
         return 0
 
@@ -412,6 +471,7 @@
             pltpu.VMEM((PARTS, per, layers, 4, rows, LANES), f32),
             pltpu.VMEM((PARTS, Q, per, rows, LANES), f32),
             pltpu.VMEM((PARTS - 1, Q, per, rows, LANES), f32),
+            pltpu.VMEM((PASSED, per - 1, rows, LANES), f32),
             pltpu.VMEM((per, Q, rows, LANES), f32),
             pltpu.VMEM((nz, rows, LANES), f32),
             pltpu.VMEM((nz, rows, LANES), f32),
@@ -423,6 +483,8 @@
             dma((2, PARTS)),
             dma((PARTS - 1, Q)),
             dma((PARTS - 1, Q)),
+            dma((2, PASSED)),
+            dma((2, PASSED)),
             dma((per, Q)),
             dma((per, Q)),
             dma((nz,)),

time: 41.1 us -> 43.1 us (1.049); the launches traced: 41 us -> 42.4 us
  Pallas kernels: 40.4 us -> 41.7 us
    pallas_call x1, Pallas kernels: 40.4 us -> 41.7 us  [local(): pl.pallas_call(functools.partial(kernel, nx, ny, 1.5 / (layers * nx)), ou...]
where the time goes in v6:
time: 43.1 us; the launch traced here: 42.4 us
  Pallas kernels  41.7 us (97%)
  local copies, waits for them, and re-layouts  0.62 us (1%)
    pallas_call x1, Pallas kernels, local(): pl.pallas_call(functools.partial(kernel, nx, ny, 1.5 / (layers * nx)), ou...  41.7 us

profile of v6, /device:TPU:6, one launch (start us, length us, event | category | flops | bytes accessed | tf_op | source)
XLA Modules:
  0.0 42.4 jit_solution(4092837322037084625)
XLA Ops:
  0.0 41.7 %shard_map.64 = f32[4,24,32]{2,1,0:T(8,128)S(1)} custom-call(f32[8,24,2048]{2,1,0:T(8,128)} %density.1, f32[8]{0:T(128)} %rest_0_.1, f32[8]{0:T(128)} %rest_1_.1, f32[8]{0:T(128)} %rest_2_.1, f32[3,8]{1,0:T(4,128)} %rest_3_.1, f32[3]{0:T(128)} %rest_4_.1), custom_call_target="tpu_custom_call" | custom-call | flops 51118080 | bytes 1572864 | tf_op jit(solution)/shard_map/pallas_call | solution.py:459
  41.7 0.6 %copy.8 = f32[4,24,32]{2,1,0:T(8,128)} copy(f32[4,24,32]{2,1,0:T(8,128)S(1)} %shard_map.64) | data formatting | bytes 24576

commit v7 on v5

--- a/solution.py
+++ b/solution.py
@@ -11,6 +11,7 @@
 MESH = pl.DeviceIdType.MESH
 LANES = 128
 Q = 4
+DEEP = 256
 G = LANES // Q
 PARTS = 8
 LEAD = 2
@@ -56,8 +57,8 @@
 ):
     given, rest = rest[:5], rest[5:]
     out, centers, widths, weights, colors, light = rest[:6]
-    x, rows_out, rows_in, depth_in, prm, emi, p1s, p1r, lastr, p2s, p2r = rest[6:17]
-    x_sem, given_sem, rows_ss, rows_rs, depth_ss, depth_rs, p1_ss, p1_rs, last_ss, last_rs, p2_ss, p2_rs = rest[17:]
+    x, rows_out, rows_in, depth_in, prm, mix, emi, p1s, p1r, lastr, p2s, p2r = rest[6:18]
+    x_sem, given_sem, rows_ss, rows_rs, depth_ss, depth_rs, p1_ss, p1_rs, last_ss, last_rs, p2_ss, p2_rs = rest[18:]
     layers, rows, cols = density.shape
     nz = nx // Q
     bumps = centers.shape[0]
@@ -162,14 +163,24 @@
     tile = (8, LANES)
     scale = math.sqrt(math.log2(math.e))
     for k in range(bumps):
-        weight = jnp.full(tile, weights[k] * step_size, jnp.float32)
-        prm[6 * k] = jnp.full(tile, centers[k], jnp.float32)
-        prm[6 * k + 1] = scale / jnp.full(tile, widths[k], jnp.float32)
-        prm[6 * k + 2] = jnp.log2(weight)
-        for c in range(3):
-            prm[6 * k + 3 + c] = jnp.full(tile, colors[c, k], jnp.float32) / weight
+        inverse = scale / jnp.full(tile, widths[k], jnp.float32)
+        prm[2 * k] = jnp.full(tile, centers[k], jnp.float32)
+        prm[2 * k + 1] = -inverse * inverse
     for c in range(3):
-        prm[6 * bumps + c] = jnp.full(tile, 0.5 * light[c], jnp.float32)
+        prm[2 * bumps + c] = jnp.full(tile, 0.5 * light[c], jnp.float32)
+    into = lax.broadcasted_iota(jnp.int32, (rows, DEEP), 0)
+    out_of = lax.broadcasted_iota(jnp.int32, (rows, DEEP), 1)
+    lines = []
+    for c in range(4):
+        line = jnp.zeros((rows, DEEP), jnp.float32)
+        for k in range(bumps):
+            factor = weights[k] * step_size if c == 0 else colors[c - 1, k] * 0.375
+            line = jnp.where(out_of == into + k * rows, factor, line)
+        lines.append(line)
+    exact = jnp.concatenate(lines, 0)
+    high = exact.astype(jnp.bfloat16)
+    mix[: 4 * rows] = high
+    mix[4 * rows :] = (exact - high.astype(jnp.float32)).astype(jnp.bfloat16)
 
     load.wait()
     for l in range(layers):
@@ -194,18 +205,28 @@
     def column_of(s, i):
         return pl.multiple_of(part_at(s, z) * width + i * LANES, LANES)
 
-    def emit_layer(s, i, at, l):
-        cells = x[l, :, pl.ds(pl.multiple_of(at + LANES, LANES), LANES)]
-        sums = None
+    def broad(i):
+        return jnp.concatenate([wide(i)] * per, 1)
+
+    def emit_layer(s, l):
+        cells = x[l, :, pl.ds(pl.multiple_of(part_at(s, z) * width + LANES, LANES), width)]
+        stack = []
         for k in range(bumps):
-            scaled = (cells - wide(6 * k)) * wide(6 * k + 1)
-            step = jnp.exp2(wide(6 * k + 2) - scaled * scaled)
-            terms = [step] + [step * wide(6 * k + 3 + c) for c in range(3)]
-            sums = terms if sums is None else [a + b for a, b in zip(sums, terms)]
-        t = sums[0]
+            away = cells - broad(2 * k)
+            stack.append(jnp.exp2(away * away * broad(2 * k + 1)))
+        if DEEP > bumps * rows:
+            stack.append(jnp.zeros((DEEP - bumps * rows, width), jnp.float32))
+        exact = jnp.concatenate(stack, 0)
+        high = exact.astype(jnp.bfloat16)
+        low = (exact - high.astype(jnp.float32)).astype(jnp.bfloat16)
+        most = jnp.dot(mix[...], high, preferred_element_type=jnp.float32)
+        rest = jnp.dot(mix[: 4 * rows], low, preferred_element_type=jnp.float32)
+        sums = most[: 4 * rows] + (most[4 * rows :] + rest)
+        t = sums[:rows]
         opacity = t * (1.0 - t * (0.5 - t * (1.0 / 6.0 - t * (1.0 / 24.0))))
-        for c, v in enumerate([opacity] + sums[1:]):
-            emi[s, i, l, c] = v
+        emi[s, l, 0] = opacity
+        for c in range(1, 4):
+            emi[s, l, c] = sums[c * rows : (c + 1) * rows]
 
     def march_layer(s, i, at, l, state):
         clear, opaque, colour = state
@@ -225,16 +246,17 @@
         ahead = [shifted([t], -1, e, lane, 1)[0] for t, e in zip(tiles, right)]
         above = shifted(tiles, 1, over_row, row, 0)
         below = shifted(tiles, -1, under_row, row, 0)
-        hx, hy, hz = (wide(6 * bumps + c) for c in range(3))
+        hx, hy, hz = (wide(2 * bumps + c) for c in range(3))
         facing = (
             hx * (after - before)
             + hy * jnp.concatenate([b - a for a, b in zip(above, below)], 0)
             + hz * jnp.concatenate([b - a for a, b in zip(behind, ahead)], 0)
         )
-        shading = 0.625 + 0.375 * jnp.tanh(facing)
-        seen = clear * emi[s, i, l, 0]
+        shading = 5.0 / 3.0 + jnp.tanh(facing)
+        local = pl.ds(pl.multiple_of(i * LANES, LANES), LANES)
+        seen = clear * emi[s, l, 0, :, local]
         lit = seen * shading
-        return clear - seen, opaque + seen, [colour[c] + lit * emi[s, i, l, c + 1] for c in range(3)]
+        return clear - seen, opaque + seen, [colour[c] + lit * emi[s, l, c + 1, :, local] for c in range(3)]
 
     def march_end(s, i, state):
         owned = regroup(state[2] + [state[1]], lane_all)
@@ -246,13 +268,11 @@
 
     def emit(s):
         def one(n, _):
-            i, l = lax.rem(n, per), n // per * 2
-            at = column_of(s, i)
-            emit_layer(s, i, at, l)
-            emit_layer(s, i, at, l + 1)
+            for l in range(layers // per):
+                emit_layer(s, n * (layers // per) + l)
             return 0
 
-        lax.fori_loop(0, per * layers // 2, one, 0)
+        lax.fori_loop(0, per, one, 0)
 
     def march(s):
         def one(i, _):
@@ -266,9 +286,10 @@
 
     def emit_and_march(e, s):
         def one(i, _):
-            emit_at, at, state = column_of(e, i), column_of(s, i), fresh
+            at, state = column_of(s, i), fresh
             for l in range(layers):
-                emit_layer(e, i, emit_at, l)
+                if l % per == 0:
+                    emit_layer(e, i * (layers // per) + l // per)
                 state = march_layer(s, i, at, l, state)
             march_end(s, i, state)
             return 0
@@ -408,8 +429,9 @@
             pltpu.VMEM((2, layers, cols), f32),
             pltpu.VMEM((2, layers, cols), f32),
             pltpu.VMEM((2, rows, cols), f32),
-            pltpu.VMEM((6 * bumps + 3, 8, LANES), f32),
-            pltpu.VMEM((PARTS, per, layers, 4, rows, LANES), f32),
+            pltpu.VMEM((2 * bumps + 3, 8, LANES), f32),
+            pltpu.VMEM((8 * rows, DEEP), jnp.bfloat16),
+            pltpu.VMEM((PARTS, layers, 4, rows, width), f32),
             pltpu.VMEM((PARTS, Q, per, rows, LANES), f32),
             pltpu.VMEM((PARTS - 1, Q, per, rows, LANES), f32),
             pltpu.VMEM((per, Q, rows, LANES), f32),

time: 41.1 us -> 41.1 us (level)
  no operation moved by 1% of the time
where the time goes in v7:
time: 41.1 us; the launch traced here: 40.9 us
  Pallas kernels  40.3 us (98%)
  local copies, waits for them, and re-layouts  0.62 us (2%)
    pallas_call x1, Pallas kernels, local(): pl.pallas_call(functools.partial(kernel, nx, ny, 1.5 / (layers * nx)), ou...  40.3 us

profile of v7, /device:TPU:6, one launch (start us, length us, event | category | flops | bytes accessed | tf_op | source)
XLA Modules:
  0.0 40.9 jit_solution(7801237516467246564)
XLA Ops:
  0.0 40.3 %shard_map.64 = f32[4,24,32]{2,1,0:T(8,128)S(1)} custom-call(f32[8,24,2048]{2,1,0:T(8,128)} %density.1, f32[8]{0:T(128)} %rest_0_.1, f32[8]{0:T(128)} %rest_1_.1, f32[8]{0:T(128)} %rest_2_.1, f32[3,8]{1,0:T(4,128)} %rest_3_.1, f32[3]{0:T(128)} %rest_4_.1), custom_call_target="tpu_custom_call" | custom-call | flops 51118080 | bytes 1572864 | tf_op jit(solution)/shard_map/pallas_call | solution.py:421
  40.3 0.6 %copy.8 = f32[4,24,32]{2,1,0:T(8,128)} copy(f32[4,24,32]{2,1,0:T(8,128)S(1)} %shard_map.64) | data formatting | bytes 24576

commit v8 on v7

--- a/solution.py
+++ b/solution.py
@@ -14,7 +14,7 @@
 DEEP = 256
 G = LANES // Q
 PARTS = 8
-LEAD = 2
+LEAD = 3
 
 
 def roll_lanes(v, by):
@@ -320,35 +320,44 @@
         rows_copy(side).wait_recv()
 
 
+    last = PARTS - 1
+
+    def halos_in(s):
+        for side in range(2):
+            depth_copy(side, s, z, (nxt, prv)[side]).wait_recv()
+
     def step(s, _):
-        @pl.when(s < PARTS)
+        @pl.when(s < last)
         def _():
-            for side in range(2):
-                depth_copy(side, s, z, (nxt, prv)[side]).wait_recv()
-
-        @pl.when(s + LEAD < PARTS)
-        def _():
-            emit_and_march(s + LEAD, s)
-
-        @pl.when((s + LEAD >= PARTS) & (s < PARTS))
-        def _():
-            march(s)
-
-        @pl.when(s < PARTS - 1)
-        def _():
+            halos_in(s)
+
+            @pl.when(s + LEAD < last)
+            def _():
+                emit_and_march(s + LEAD, s)
+
+            @pl.when(s + LEAD >= last)
+            def _():
+                march(s)
+
             for k in (2, 1, 3):
                 p1_copy(s, k).start()
 
-        @pl.when(s == PARTS - 1)
+        @pl.when(s == last)
         def _():
+            emit(last)
+
+        @pl.when(s == last + 1)
+        def _():
+            halos_in(last)
+            march(last)
             for g in range(per):
                 for k in range(Q):
                     if (g, k) != (0, 0):
                         last_copy(g, k).start()
 
-        @pl.when(s >= 2)
+        @pl.when((s == LEAD) | (s >= last - 1))
         def _():
-            t = s - 2
+            t = jnp.where(s == LEAD, 0, s - (last - 2))
             first = part_at(t, z) * per
             p1r[t, 0] = p1s[t, y]
             for k in range(1, Q):
@@ -365,7 +374,7 @@
 
         return 0
 
-    lax.fori_loop(0, PARTS + 1, step, 0)
+    lax.fori_loop(0, 2 * last - 2, step, 0)
 
     for side in range(2):
         rows_copy(side).wait_send()

time: 41.1 us -> 40.9 us (level)
  no operation moved by 1% of the time
where the time goes in v8:
time: 40.9 us; the launch traced here: 40.6 us
  Pallas kernels  40 us (98%)
  local copies, waits for them, and re-layouts  0.62 us (2%)
    pallas_call x1, Pallas kernels, local(): pl.pallas_call(functools.partial(kernel, nx, ny, 1.5 / (layers * nx)), ou...  40 us

profile of v8, /device:TPU:6, one launch (start us, length us, event | category | flops | bytes accessed | tf_op | source)
XLA Modules:
  0.0 40.6 jit_solution(12288864862245723971)
XLA Ops:
  0.0 40.0 %shard_map.64 = f32[4,24,32]{2,1,0:T(8,128)S(1)} custom-call(f32[8,24,2048]{2,1,0:T(8,128)} %density.1, f32[8]{0:T(128)} %rest_0_.1, f32[8]{0:T(128)} %rest_1_.1, f32[8]{0:T(128)} %rest_2_.1, f32[3,8]{1,0:T(4,128)} %rest_3_.1, f32[3]{0:T(128)} %rest_4_.1), custom_call_target="tpu_custom_call" | custom-call | flops 51118080 | bytes 1572864 | tf_op jit(solution)/shard_map/pallas_call | solution.py:430
  40.0 0.6 %copy.8 = f32[4,24,32]{2,1,0:T(8,128)} copy(f32[4,24,32]{2,1,0:T(8,128)S(1)} %shard_map.64) | data formatting | bytes 24576

commit v9 on v8

--- a/solution.py
+++ b/solution.py
@@ -157,6 +157,15 @@
             device_id=(to * Q + y, my),
             device_id_type=MESH,
         )
+
+    pl.semaphore_wait(barrier, 4 + (nz - 1) + per * (Q - 1))
+
+    def send_depth(s, _):
+        depth_copy(0, s, nxt // Q, nxt).start()
+        depth_copy(1, s, prv // Q, prv).start()
+        return 0
+
+    lax.fori_loop(0, PARTS, send_depth, 0)
 
     for fetch in fetches:
         fetch.wait()
@@ -186,6 +195,8 @@
     for l in range(layers):
         rows_out[0, l : l + 1, :] = x[l, 0:1, LANES : LANES + cols]
         rows_out[1, l : l + 1, :] = x[l, rows - 1 : rows, LANES : LANES + cols]
+    for side in range(2):
+        rows_copy(side).start()
 
     lane = lax.broadcasted_iota(jnp.int32, tile, 1)
     row = lax.broadcasted_iota(jnp.int32, tile, 0)
@@ -296,26 +307,9 @@
 
         lax.fori_loop(0, per, one, 0)
 
-    emit(0)
-    pl.semaphore_wait(barrier, 4 + (nz - 1) + per * (Q - 1))
-
-    def send_depth(s):
-        depth_copy(0, s, nxt // Q, nxt).start()
-        depth_copy(1, s, prv // Q, prv).start()
-
-    send_depth(0)
-    for side in range(2):
-        rows_copy(side).start()
-    for s in range(1, LEAD):
-        send_depth(s)
-    for s in range(1, LEAD):
+
+    for s in range(LEAD):
         emit(s)
-
-    def send_more(s, _):
-        send_depth(s)
-        return 0
-
-    lax.fori_loop(LEAD, PARTS, send_more, 0)
     for side in range(2):
         rows_copy(side).wait_recv()
 

time: 40.9 us -> 40.8 us (level)
  no operation moved by 1% of the time
where the time goes in v9:
time: 40.8 us; the launch traced here: 40.4 us
  Pallas kernels  39.8 us (98%)
  local copies, waits for them, and re-layouts  0.62 us (2%)
    pallas_call x1, Pallas kernels, local(): pl.pallas_call(functools.partial(kernel, nx, ny, 1.5 / (layers * nx)), ou...  39.8 us

profile of v9, /device:TPU:6, one launch (start us, length us, event | category | flops | bytes accessed | tf_op | source)
XLA Modules:
  0.0 40.4 jit_solution(16804049078798352012)
XLA Ops:
  0.0 39.8 %shard_map.64 = f32[4,24,32]{2,1,0:T(8,128)S(1)} custom-call(f32[8,24,2048]{2,1,0:T(8,128)} %density.1, f32[8]{0:T(128)} %rest_0_.1, f32[8]{0:T(128)} %rest_1_.1, f32[8]{0:T(128)} %rest_2_.1, f32[3,8]{1,0:T(4,128)} %rest_3_.1, f32[3]{0:T(128)} %rest_4_.1), custom_call_target="tpu_custom_call" | custom-call | flops 51118080 | bytes 1572864 | tf_op jit(solution)/shard_map/pallas_call | solution.py:424
  39.8 0.6 %copy.8 = f32[4,24,32]{2,1,0:T(8,128)} copy(f32[4,24,32]{2,1,0:T(8,128)S(1)} %shard_map.64) | data formatting | bytes 24576

commit v10 on v7

--- a/solution.py
+++ b/solution.py
@@ -11,6 +11,7 @@
 MESH = pl.DeviceIdType.MESH
 LANES = 128
 Q = 4
+STRAIGHT = 3
 DEEP = 256
 G = LANES // Q
 PARTS = 8
@@ -94,9 +95,10 @@
         return 0
 
     lax.fori_loop(1, nz, greet_z, 0)
-    for k in range(1, Q):
-        for g in range(per):
-            greet((first_z + lax.rem(in_group + g, per)) * Q + lax.rem(y + k, Q), my)
+    for off in (0, per, nz - per):
+        for k in range(1, Q):
+            for g in range(per):
+                greet(lax.rem(first_z + off + g, nz) * Q + lax.rem(y + k, Q), my)
     x[:, :, :LANES] = jnp.zeros((layers, rows, LANES), jnp.float32)
     x[:, :, LANES + cols :] = jnp.zeros((layers, rows, LANES), jnp.float32)
 
@@ -136,16 +138,20 @@
             device_id_type=MESH,
         )
 
-    def last_copy(g, k):
+    def last_copy(s, g, k):
         at, to = lax.rem(in_group + g, per), lax.rem(y + k, Q)
+        d = s - (PARTS - STRAIGHT)
         return pltpu.make_async_remote_copy(
-            src_ref=p1s.at[PARTS - 1, to, at],
-            dst_ref=lastr.at[g, k],
-            send_sem=last_ss.at[g, k],
-            recv_sem=last_rs.at[g, k],
-            device_id=((first_z + at) * Q + to, my),
+            src_ref=p1s.at[s, to, at],
+            dst_ref=lastr.at[d, g, k],
+            send_sem=last_ss.at[d, g, k],
+            recv_sem=last_rs.at[d, g, k],
+            device_id=((part_at(s, z) * per + at) * Q + to, my),
             device_id_type=MESH,
         )
+
+    def from_first(s):
+        return lax.rem(2 * (z // per) - part_at(s, z) + 2 * PARTS, PARTS) * per
 
     def p2_copy(k):
         to = lax.rem(z + k, nz)
@@ -297,7 +303,7 @@
         lax.fori_loop(0, per, one, 0)
 
     emit(0)
-    pl.semaphore_wait(barrier, 4 + (nz - 1) + per * (Q - 1))
+    pl.semaphore_wait(barrier, 4 + (nz - 1) + 3 * per * (Q - 1))
 
     def send_depth(s):
         depth_copy(0, s, nxt // Q, nxt).start()
@@ -334,19 +340,23 @@
         def _():
             march(s)
 
-        @pl.when(s < PARTS - 1)
+        @pl.when(s < PARTS - STRAIGHT)
         def _():
             for k in (2, 1, 3):
                 p1_copy(s, k).start()
 
-        @pl.when(s == PARTS - 1)
-        def _():
+        @pl.when(s >= PARTS - STRAIGHT)
+        def _():
+            @pl.when(s < PARTS - 1)
+            def _():
+                last_copy(s, 0, 0).start()
+
             for g in range(per):
                 for k in range(Q):
                     if (g, k) != (0, 0):
-                        last_copy(g, k).start()
-
-        @pl.when(s >= 2)
+                        last_copy(s, g, k).start()
+
+        @pl.when((s >= 2) & (s < PARTS - STRAIGHT + 2))
         def _():
             t = s - 2
             first = part_at(t, z) * per
@@ -365,7 +375,7 @@
 
         return 0
 
-    lax.fori_loop(0, PARTS + 1, step, 0)
+    lax.fori_loop(0, PARTS, step, 0)
 
     for side in range(2):
         rows_copy(side).wait_send()
@@ -374,7 +384,7 @@
         for side in range(2):
             depth_copy(side, s, z, (nxt, prv)[side]).wait_send()
 
-        @pl.when(s < PARTS - 1)
+        @pl.when(s < PARTS - STRAIGHT)
         def _():
             for k in range(1, Q):
                 p1_copy(s, k).wait_send()
@@ -383,25 +393,36 @@
 
     lax.fori_loop(0, PARTS, finish, 0)
 
-    lastr[0, 0] = p1s[PARTS - 1, y, in_group]
-    for g in range(per):
-        for k in range(Q):
-            if (g, k) != (0, 0):
-                last_copy(g, k).wait()
-    for g in range(per):
-        near = lax.rem(in_group + per - g, per)
-        total = lastr[near, lax.rem(y + 1, Q)]
-        for j in range(Q - 2, -1, -1):
-            total = over(lastr[near, lax.rem(y + Q - j, Q)], total, lane_all)
-        p2r[lax.rem(z + nz - (first_z + g), nz)] = total
-
-    def finish_p2(i, _):
-        other = lax.rem(first_z + i, nz)
-        p2_copy(lax.rem(other + nz - z, nz)).wait_send()
-        p2_copy(lax.rem(z + nz - other, nz)).wait_recv()
-        return 0
-
-    lax.fori_loop(per, nz, finish_p2, 0)
+    lastr[STRAIGHT - 1, 0, 0] = p1s[PARTS - 1, y, in_group]
+
+    def join_last(d, _):
+        s = d + PARTS - STRAIGHT
+
+        @pl.when(s < PARTS - 1)
+        def _():
+            last_copy(s, 0, 0).wait()
+
+        for g in range(per):
+            for k in range(Q):
+                if (g, k) != (0, 0):
+                    last_copy(s, g, k).wait()
+        for g in range(per):
+            near = lax.rem(in_group + per - g, per)
+            total = lastr[d, near, lax.rem(y + 1, Q)]
+            for j in range(Q - 2, -1, -1):
+                total = over(lastr[d, near, lax.rem(y + Q - j, Q)], total, lane_all)
+            p2r[lax.rem(z + nz - (from_first(s) + g), nz)] = total
+        return 0
+
+    lax.fori_loop(0, STRAIGHT, join_last, 0)
+
+    def finish_p2(s, _):
+        for g in range(per):
+            p2_copy(lax.rem(part_at(s, z) * per + g + nz - z, nz)).wait_send()
+            p2_copy(lax.rem(z + nz - (from_first(s) + g), nz)).wait_recv()
+        return 0
+
+    lax.fori_loop(0, PARTS - STRAIGHT, finish_p2, 0)
 
     total = p2r[lax.rem(z + 1, nz)]
     for i in range(1, nz):
@@ -434,7 +455,7 @@
             pltpu.VMEM((PARTS, layers, 4, rows, width), f32),
             pltpu.VMEM((PARTS, Q, per, rows, LANES), f32),
             pltpu.VMEM((PARTS - 1, Q, per, rows, LANES), f32),
-            pltpu.VMEM((per, Q, rows, LANES), f32),
+            pltpu.VMEM((STRAIGHT, per, Q, rows, LANES), f32),
             pltpu.VMEM((nz, rows, LANES), f32),
             pltpu.VMEM((nz, rows, LANES), f32),
             dma,
@@ -445,8 +466,8 @@
             dma((2, PARTS)),
             dma((PARTS - 1, Q)),
             dma((PARTS - 1, Q)),
-            dma((per, Q)),
-            dma((per, Q)),
+            dma((STRAIGHT, per, Q)),
+            dma((STRAIGHT, per, Q)),
             dma((nz,)),
             dma((nz,)),
         ],

time: 41.1 us -> 44.1 us (1.073)
  Pallas kernels: 40.3 us -> 43 us
    pallas_call x1, Pallas kernels: 40.3 us -> 43 us  [local(): pl.pallas_call(functools.partial(kernel, nx, ny, 1.5 / (layers * nx)), ou...]
where the time goes in v10:
time: 44.1 us; the launch traced here: 43.6 us
  Pallas kernels  43 us (98%)
  local copies, waits for them, and re-layouts  0.62 us (1%)
    pallas_call x1, Pallas kernels, local(): pl.pallas_call(functools.partial(kernel, nx, ny, 1.5 / (layers * nx)), ou...  43 us

profile of v10, /device:TPU:6, one launch (start us, length us, event | category | flops | bytes accessed | tf_op | source)
XLA Modules:
  0.0 43.6 jit_solution(3283275311111698541)
XLA Ops:
  0.0 43.0 %shard_map.64 = f32[4,24,32]{2,1,0:T(8,128)S(1)} custom-call(f32[8,24,2048]{2,1,0:T(8,128)} %density.1, f32[8]{0:T(128)} %rest_0_.1, f32[8]{0:T(128)} %rest_1_.1, f32[8]{0:T(128)} %rest_2_.1, f32[3,8]{1,0:T(4,128)} %rest_3_.1, f32[3]{0:T(128)} %rest_4_.1), custom_call_target="tpu_custom_call" | custom-call | flops 51118080 | bytes 1572864 | tf_op jit(solution)/shard_map/pallas_call | solution.py:442
  43.0 0.6 %copy.8 = f32[4,24,32]{2,1,0:T(8,128)} copy(f32[4,24,32]{2,1,0:T(8,128)S(1)} %shard_map.64) | data formatting | bytes 24576
